TPU v7x, 32 devices: a whole 2x2x4 slice. The times are simulated.
32 devices in a mesh: dp: 8 (over z, y), inner: 4 (over x, core).
Axes of the slice: x: 2, y: 2, z: 4, core: 2. Of those that a mesh axis runs over, the one named last changes fastest.
Arguments:
- inputs: bfloat16 [32768, 768], P(('dp', 'inner')), may hold values from -6 to 6
- qkv_weight: bfloat16 [1769472], P(('dp', 'inner')), may hold values from -0.21875 to 0.21875
- out_weight: bfloat16 [589824], P(('dp', 'inner')), may hold values from -0.625 to 0.625
- up_weight: bfloat16 [2359296], P(('dp', 'inner')), may hold values from -0.21875 to 0.21875
- down_weight: bfloat16 [2359296], P(('dp', 'inner')), may hold values from -0.109375 to 0.109375
- vectors: bfloat16 [9216], P(('dp', 'inner')), may hold values from -1 to 2
- lengths: int32 [64], P(('dp', 'inner')), may hold values from 128 to 512, as said below
- counts: int32 [64], P(('dp', 'inner')), may hold values from 42 to 128, as said below
- positions: int32 [64, 128], P(('dp', 'inner')), may hold values from 0 to 511, as said below
- grad_values: bfloat16 [64, 128, 768], P(('dp', 'inner')), may hold values from -6 to 6
Outputs:
- layer_out: bfloat16 [32768, 768], P(('dp', 'inner'))
- input_grad: bfloat16 [32768, 768], P(('dp', 'inner'))
- qkv_grad: float32 [1769472], P(('dp', 'inner'))
- attn_out_grad: float32 [589824], P(('dp', 'inner'))
- up_weight_gradient: float32 [2359296], P(('dp', 'inner'))
- down_grad: float32 [2359296], P(('dp', 'inner'))
- vector_grad: float32 [9216], P(('dp', 'inner'))
Inputs may be any that keep to these rules, and one draw needn't show every extreme that they name: `lengths`: some sequence has all 512 tokens valid and some has exactly 128. counts[s] is at most lengths[s]; some sequence uses all 128 slots. Each row holds distinct positions, all below that sequence's length.
All inputs are finite; a program needn't handle non-finite values.
Results may differ from a plain program's by a relative error of at most 0.012.
Values may be sent and summed in bfloat16 or wider, within the bound.
A program may use at most 192 MiB of HBM per device.

v0:
```python
from functools import partial

import jax
import jax.numpy as jnp
from jax import lax
from jax.sharding import PartitionSpec as P

D = 768
H = 12
HD = 64
FF = 3072
SEQ_LEN = 512
PMAX = 128


norm_eps = 1e-05
masked_score = -1e30


def layer_norm(row_data, gain_row, shift_row):
    mean_row = jnp.mean(row_data, -1, keepdims=True)
    centered = row_data - mean_row
    spread = jnp.mean(centered * centered, -1, keepdims=True)
    return centered * lax.rsqrt(spread + norm_eps) * gain_row + shift_row


def split_vectors(vector_in):
    starts = [0, D, 2 * D, 3 * D, 4 * D, 5 * D, 5 * D + FF, 6 * D + FF, 7 * D + FF, 8 * D + FF]
    return tuple(
        (vector_in[starts[item_count] : starts[item_count + 1]] for item_count in range(9))
    )


def matmul(left, right):
    return jnp.dot(left, right, preferred_element_type=jnp.float32)


def contracted_row_axes(left, right):
    return lax.dot_general(
        left, right, (((0,), (0,)), ((), ())), preferred_element_type=jnp.float32
    )


def contract_cols(left, right):
    return lax.dot_general(
        left, right, (((1,), (1,)), ((), ())), preferred_element_type=jnp.float32
    )


def masked_scores(head_rows, key_valid):
    queries = head_rows[:, 0]
    keys_in = head_rows[:, 1]
    scores = jnp.einsum(
        "qhd,khd->hqk", queries, keys_in, preferred_element_type=jnp.float32
    ) * HD ** (-0.5)
    return jnp.where(key_valid[None, None, :], scores, masked_score)


def attend_forward(items):
    head_rows, key_valid = items
    scores = masked_scores(head_rows, key_valid)
    row_max = jnp.max(scores, -1, keepdims=True)
    exponent = jnp.exp(scores - row_max)
    row_total = jnp.sum(exponent, -1, keepdims=True)
    attn_probs = (exponent / row_total).astype(jnp.bfloat16)
    context = jnp.einsum(
        "hqk,khd->qhd", attn_probs, head_rows[:, 2], preferred_element_type=jnp.float32
    )
    return (context.reshape(SEQ_LEN, D), row_max + jnp.log(row_total))


def attend_backward(items):
    head_rows, key_valid, log_norm, ctx_grad = items
    queries = head_rows[:, 0]
    keys_in = head_rows[:, 1]
    value_entries = head_rows[:, 2]
    attn_probs = jnp.exp(masked_scores(head_rows, key_valid) - log_norm)
    probs_low = attn_probs.astype(jnp.bfloat16)
    prob_grad = jnp.einsum(
        "qhd,khd->hqk", ctx_grad, value_entries, preferred_element_type=jnp.float32
    )
    value_grad = jnp.einsum("hqk,qhd->khd", probs_low, ctx_grad, preferred_element_type=jnp.float32)
    row_dot = jnp.sum(prob_grad * attn_probs, -1, keepdims=True)
    score_grad = (attn_probs * (prob_grad - row_dot)).astype(jnp.bfloat16)
    query_grad = jnp.einsum(
        "hqk,khd->qhd", score_grad, keys_in, preferred_element_type=jnp.float32
    ) * HD ** (-0.5)
    key_grad = jnp.einsum(
        "hqk,qhd->khd", score_grad, queries, preferred_element_type=jnp.float32
    ) * HD ** (-0.5)
    stacked = jnp.stack([query_grad, key_grad, value_grad], 1)
    return stacked.reshape(SEQ_LEN, 3 * D).astype(jnp.bfloat16)


def on_device(
    inputs,
    qkv_weight,
    out_weight,
    up_weight,
    down_weight,
    vectors,
    lengths,
    counts,
    positions,
    grad_values,
):
    attn_parts = (
        lax.all_gather(qkv_weight, ("dp", "inner"), axis=0, tiled=True),
        lax.all_gather(out_weight, ("dp", "inner"), axis=0, tiled=True),
        lax.all_gather(vectors, ("dp", "inner"), axis=0, tiled=True),
    )
    ffn_parts = (
        lax.all_gather(up_weight, ("dp", "inner"), axis=0, tiled=True),
        lax.all_gather(down_weight, ("dp", "inner"), axis=0, tiled=True),
    )
    qkv_matrix = attn_parts[0].reshape(D, 3 * D)
    output_projection = attn_parts[1].reshape(D, D)
    q_bias, v_bias, out_bias, gain_one, shift_one, up_bias, down_bias, gain_two, shift_two = (
        split_vectors(attn_parts[2].astype(jnp.float32))
    )
    up_matrix = ffn_parts[0].reshape(D, FF)
    down_matrix = ffn_parts[1].reshape(FF, D)
    groups = inputs.shape[0] // SEQ_LEN
    qkv_bias = jnp.concatenate([q_bias, jnp.zeros_like(q_bias), v_bias])
    joined = (matmul(inputs, qkv_matrix) + qkv_bias).astype(jnp.bfloat16)
    split_heads = joined.reshape(groups, SEQ_LEN, 3, H, HD)
    key_valid = lax.broadcasted_iota(jnp.int32, (groups, SEQ_LEN), 1) < lengths[:, None]
    context, log_norm = lax.map(attend_forward, (split_heads, key_valid))
    context_low = context.reshape(groups * SEQ_LEN, D).astype(jnp.bfloat16)
    attn_out = matmul(context_low, output_projection) + out_bias
    resid_one = inputs.astype(jnp.float32) + attn_out
    normed_one, first_pull = jax.vjp(layer_norm, resid_one, gain_one, shift_one)
    normed_low = normed_one.astype(jnp.bfloat16)
    pre_act = matmul(normed_low, up_matrix) + up_bias
    gelu_exact = partial(jax.nn.gelu, approximate=False)
    activated, gelu_pull = jax.vjp(gelu_exact, pre_act)
    active_low = activated.astype(jnp.bfloat16)
    ffn_out = matmul(active_low, down_matrix) + down_bias
    layer_out, second_pull = jax.vjp(layer_norm, normed_one + ffn_out, gain_two, shift_two)
    places = jnp.arange(SEQ_LEN, dtype=jnp.int32)
    slot_ids = jnp.arange(PMAX, dtype=jnp.int32)
    matches = (positions[:, :, None] == places[None, None, :]) & (
        slot_ids[None, :, None] < counts[:, None, None]
    )
    cotangent = jnp.einsum(
        "jgw,jgq->jwq",
        matches.astype(jnp.bfloat16),
        grad_values,
        preferred_element_type=jnp.float32,
    ).reshape(-1, D)
    d_two, gain_two_grad, shift_two_grad = second_pull(cotangent)
    ffn_back = (
        lax.all_gather(up_weight, ("dp", "inner"), axis=0, tiled=True),
        lax.all_gather(down_weight, ("dp", "inner"), axis=0, tiled=True),
    )
    up_matrix = ffn_back[0].reshape(D, FF)
    down_matrix = ffn_back[1].reshape(FF, D)
    ffn_grad = d_two.astype(jnp.bfloat16)
    down_grad = contracted_row_axes(active_low, ffn_grad)
    down_bias_grad = jnp.sum(ffn_grad.astype(jnp.float32), 0)
    act_grad = contract_cols(ffn_grad, down_matrix)
    pre_grad = gelu_pull(act_grad)[0].astype(jnp.bfloat16)
    up_weight_gradient = contracted_row_axes(normed_low, pre_grad)
    up_bias_grad = jnp.sum(pre_grad.astype(jnp.float32), 0)
    d_normed = d_two + contract_cols(pre_grad, up_matrix)
    ffn_sums = (
        lax.psum_scatter(
            up_weight_gradient.reshape(-1), ("dp", "inner"), scatter_dimension=0, tiled=True
        ),
        lax.psum_scatter(down_grad.reshape(-1), ("dp", "inner"), scatter_dimension=0, tiled=True),
    )
    d_one, gain_one_grad, shift_one_grad = first_pull(d_normed)
    attn_back = (
        lax.all_gather(qkv_weight, ("dp", "inner"), axis=0, tiled=True),
        lax.all_gather(out_weight, ("dp", "inner"), axis=0, tiled=True),
    )
    qkv_matrix = attn_back[0].reshape(D, 3 * D)
    output_projection = attn_back[1].reshape(D, D)
    attn_grad = d_one.astype(jnp.bfloat16)
    out_grad = contracted_row_axes(context_low, attn_grad)
    out_bias_grad = jnp.sum(attn_grad.astype(jnp.float32), 0)
    ctx_grad = (
        contract_cols(attn_grad, output_projection)
        .astype(jnp.bfloat16)
        .reshape(groups, SEQ_LEN, H, HD)
    )
    joined_grad = lax.map(attend_backward, (split_heads, key_valid, log_norm, ctx_grad))
    joined_grad = joined_grad.reshape(groups * SEQ_LEN, 3 * D)
    qkv_grad = contracted_row_axes(inputs, joined_grad)
    joined_sums = jnp.sum(joined_grad.astype(jnp.float32), 0)
    input_grad = (d_one + contract_cols(joined_grad, qkv_matrix)).astype(jnp.bfloat16)
    vector_grad = jnp.concatenate(
        [
            joined_sums[:D],
            joined_sums[2 * D :],
            out_bias_grad,
            gain_one_grad,
            shift_one_grad,
            up_bias_grad,
            down_bias_grad,
            gain_two_grad,
            shift_two_grad,
        ]
    )
    attn_sums = (
        lax.psum_scatter(qkv_grad.reshape(-1), ("dp", "inner"), scatter_dimension=0, tiled=True),
        lax.psum_scatter(out_grad.reshape(-1), ("dp", "inner"), scatter_dimension=0, tiled=True),
        lax.psum_scatter(vector_grad, ("dp", "inner"), scatter_dimension=0, tiled=True),
    )
    return (
        layer_out.astype(jnp.bfloat16),
        input_grad,
        attn_sums[0],
        attn_sums[1],
        ffn_sums[0],
        ffn_sums[1],
        attn_sums[2],
    )


def solution(mesh):
    placed = (
        P(("dp", "inner"), None),
        P(("dp", "inner")),
        P(("dp", "inner")),
        P(("dp", "inner")),
        P(("dp", "inner")),
        P(("dp", "inner")),
        P(("dp", "inner")),
        P(("dp", "inner")),
        P(("dp", "inner"), None),
        P(("dp", "inner"), None, None),
    )
    return jax.shard_map(
        on_device,
        mesh=mesh,
        in_specs=placed,
        out_specs=(
            P(("dp", "inner"), None),
            P(("dp", "inner"), None),
            P(("dp", "inner")),
            P(("dp", "inner")),
            P(("dp", "inner")),
            P(("dp", "inner")),
            P(("dp", "inner")),
        ),
        check_vma=False,
    )
```

profile of v0, /device:TPU:0, one launch (start us, length us, event | category | flops | bytes accessed | tf_op | source)
XLA Modules:
  0.0 892.1 jit_solution(15663479159318579448)
XLA Ops:
  11.0 42.2 %all-reduce = bf16[9216]{0:T(1024)(128)(2,1)S(1)} all-reduce(bf16[9216]{0:T(1024)(128)(2,1)S(1)} %dynamic-update-slice), channel_id=1, replica_groups=mesh['dp'=8,'inner'=4] {'dp','inner'}, use_global_device_ids=true, to_apply=%add | all-reduce | flops 9216 | bytes 36864
  62.6 5.0 all-gather.7.cloned.1.call-done
  71.0 58.6 %all-gather.5.cloned.1.call-done = bf16[1769472]{0:T(1024)(128)(2,1)} async-done(((bf16[55296]{0:T(1024)(128)(2,1)}), bf16[1769472]{0:T(1024)(128)(2,1)}) %all-gather.5.cloned.1.call-update) | async-done | bytes 3538960 | tf_op jit(solution)/shard_map/all_gather | solution.py:108
  129.6 7.6 reshape.194
  137.2 7.4 add_convert_fusion.1
  144.7 6.6 copy.53
  151.3 8.9 reshape.195
  160.1 5.7 copy.54
  165.8 23.8 %while.22 = (s32[]{:T(128)}, bf16[2,512,768]{2,1,0:T(8,128)(2,1)S(1)}, f32[2,12,512,1]{2,1,3,0:T(8,128)}, bf16[2,512,3,12,64]{1,4,3,2,0:T(8,128)(2,1)}, pred[2,512]{1,0:T(4,128)(4,1)S(1)}, /*index=5*/s32[]{:T(128)}) while((s32[]{:T(128)}, bf16[2,512,768]{2,1,0:T(8,128)(2,1)S(1)}, f32[2,12,512,1]{2,1,3,0:T(8,128)}, ...), condition=%wide.region_3.4_spmd, body=%wide.region_0.3_spmd.sunk | while | flops 843048960 | bytes 48983120 | solution.py:128
  195.1 8.2 reshape.197
  203.4 37.9 %multiply_convert_fusion.3 = (bf16[1024,3072]{1,0:T(8,128)(2,1)}, f32[1024,3072]{1,0:T(8,128)}, f32[1024,3072]{1,0:T(8,128)}) fusion(f32[3072]{0:T(1024)S(1)} %copy-done.26, bf16[768,3072]{1,0:T(8,128)(2,1)} %reshape.197, f32[1024,768]{0,1:T(8,128)S(1)} %get-tuple-element.179, f32[768]{0:T(1024)S(1)} %copy-done.27, f32[768]{0:T(1024)S(1)} %copy-done.17, ...), kind=kOutput, calls=%fused_computation.50 | convolution fusion | flops 5043388416 | bytes 39348224 | tf_op jit(solution)/shard_map/dot_general | solution.py:35
  241.3 19.0 %all-gather.11.cloned.1.call-done = bf16[2359296]{0:T(1024)(128)(2,1)} async-done(((bf16[73728]{0:T(1024)(128)(2,1)}), bf16[2359296]{0:T(1024)(128)(2,1)}) %all-gather.11.cloned.1.call-update) | async-done | bytes 4718608 | tf_op jit(solution)/shard_map/all_gather | solution.py:114
  260.3 9.6 %reshape.198 = bf16[3072,768]{1,0:T(8,128)(2,1)} reshape(bf16[2359296]{0:T(1024)(128)(2,1)} %all-gather.11.cloned.1.call-done) | data formatting | bytes 9437184 | tf_op jit(solution)/shard_map/reshape | solution.py:122
  269.9 8.9 %fusion.50 = (f32[1024]{0:T(1024)S(1)}, f32[1024,768]{0,1:T(8,128)S(1)}) fusion(f32[768]{0:T(1024)S(1)} %copy-done.28, bf16[1024,3072]{1,0:T(8,128)(2,1)} %get-tuple-element.163, bf16[3072,768]{1,0:T(8,128)(2,1)} %reshape.198, f32[768]{0:T(1024)S(1)} %copy-done.27, f32[768]{0:T(1024)S(1)} %copy-done.17, f32[1024]{0:T(1024)S(1)} %fusion.40, ...), kind=kOutput, calls=%fused_computation.120 | convolution fusion | flops 4837342208 | bytes 17323008 | tf_op jit(solution)/shard_map/dot_general | solution.py:35
  285.9 7.6 fusion.53
  293.6 19.2 %convert_reduce_fusion = (f32[3072]{0:T(1024)}, bf16[1024,3072]{1,0:T(8,128)(2,1)}) fusion(f32[1024,3072]{1,0:T(8,128)} %get-tuple-element.164, bf16[1024,768]{0,1:T(8,128)(2,1)} %copy-done.8, bf16[3072,768]{1,0:T(8,128)(2,1)} %reshape.198, f32[1024,3072]{1,0:T(8,128)} %get-tuple-element.180, f32[3072]{0:T(1024)S(1)} %copy-done.26), kind=kOutput, calls=%fused_computation.48 | convolution fusion | flops 4885312512 | bytes 37773312 | tf_op jit(solution)/shard_map/dot_general | solution.py:45
  312.7 10.4 %multiply_reduce_fusion.2 = (f32[768]{0:T(1024)}, f32[1024]{0:T(1024)S(1)}, f32[768]{0:T(1024)}, f32[1024,768]{0,1:T(8,128)S(1)}) fusion(f32[1024,768]{0,1:T(8,128)S(1)} %get-tuple-element.179, f32[1024]{0:T(1024)S(1)} %fusion.40, f32[1024]{0:T(1024)S(1)} %broadcast_multiply_fusion.1, f32[768]{0:T(1024)S(1)} %copy-done.17, ...), kind=kOutput, calls=%fused_computation.72 | convolution fusion | flops 4839699456 | bytes 20472832 | tf_op jit(solution)/shard_map/dot_general | solution.py:45
  323.1 7.7 convolution_bitcast_fusion.1
  340.4 52.8 %while.23 = (s32[]{:T(128)}, bf16[2,512,2304]{1,2,0:T(8,128)(2,1)}, bf16[2,512,3,12,64]{1,4,3,2,0:T(8,128)(2,1)}, pred[2,512]{1,0:T(4,128)(4,1)S(1)}, f32[2,12,5...) while((s32[]{:T(128)}, bf16[2,512,2304]{1,2,0:T(8,128)(2,1)}, ...), condition=%wide.region_14.15_spmd, body=%wide.region_12.14_spmd.sunk | while | flops 2064771072 | bytes 116583520 | solution.py:187
  344.4 7.4 multiply_reduce_fusion.8
  351.8 7.1 multiply_convert_fusion.5
  370.6 7.4 multiply_reduce_fusion.8
  378.0 7.1 multiply_convert_fusion.5
  393.2 10.8 %reshape.205 = f32[2359296]{0:T(1024)} reshape(f32[3072,768]{1,0:T(8,128)} %fusion.53) | data formatting | bytes 18874368 | tf_op jit(solution)/shard_map/reshape | solution.py:170
  404.0 9.5 %copy.91 = f32[96,24,8,128]{3,1,2,0:T(8,128)} copy(f32[96,24,8,128]{3,2,1,0:T(8,128)} %convolution_bitcast_fusion.1) | data formatting | bytes 18874368
  413.5 6.8 copy.61
  420.3 8.4 convolution_bitcast_fusion
  428.7 8.0 copy.63
  436.7 8.1 reshape.202
  448.3 9.2 %add_convert_fusion.2 = bf16[1024,768]{0,1:T(8,128)(2,1)} fusion(f32[1024,768]{0,1:T(8,128)S(1)} %copy-done.4, bf16[1024,2304]{1,0:T(8,128)(2,1)} %bitcast.141, bf16[768,2304]{1,0:T(8,128)(2,1)} %reshape.194, f32[1024]{0:T(1024)S(1)} %copy-done.23), kind=kOutput, calls=%fused_computation.74 | convolution fusion | flops 3626237952 | bytes 12980224 | tf_op jit(solution)/shard_map/dot_general | solution.py:45
  466.1 41.7 %all-reduce.5 = f32[9216]{0:T(1024)S(1)} all-reduce(f32[9216]{0:T(1024)S(1)} %constant_dynamic-update-slice_fusion.2), channel_id=6, replica_groups=mesh['dp'=8,'inner'=4] {'dp','inner'}, use_global_device_ids=true, to_apply=%region_27.28.clone | all-reduce | flops 9216 | bytes 73728
  508.4 370.2 %all-reduce.9.cloned.1.call-done = (f32[1769472]{0:T(1024)}, f32[589824]{0:T(1024)}, f32[2359296]{0:T(1024)}, f32[2359296]{0:T(1024)}) async-done(((f32[1769472]{0:T(1024)}, f32[589824]{0:T(1024)}, f32[2359296]{0:T(1024)}, f32[2359296]{0:T(1024)}), (f32[1769472]{0:T(1024)}, f32[589824]{0:T(1024)}, f32[2359296]{0:T(1024)}, f32[2359296]{0:T(1024)})) %all-reduce.9.cloned.1.call-update) | async-done | bytes 28311568
  (177 shorter events, 104.6 us)
Async XLA Ops:
  7.2 51.3 %copy-start = (bf16[2,128,768]{2,1,0:T(8,128)(2,1)S(1)}, bf16[2,128,768]{2,1,0:T(8,128)(2,1)}, u32[]{:S(2)}) copy-start(bf16[2,128,768]{2,1,0:T(8,128)(2,1)} %param.23) | copy-start | bytes 1179652
  7.2 60.5 %all-gather.7.cloned.1.call-start = ((), (), s32[]{:S(2)}) async-start(), calls=%async_computation.1 | async-start | bytes 1216512 | tf_op jit(solution)/shard_map/all_gather | solution.py:109
  7.9 121.7 %all-gather.5.cloned.1.call-start = ((), (), s32[]{:S(2)}) async-start(), calls=%async_computation | async-start | bytes 3649536 | tf_op jit(solution)/shard_map/all_gather | solution.py:108
  8.7 186.5 %all-gather.9.cloned.1.call-start = ((), (), s32[]{:S(2)}) async-start(), calls=%async_computation.2 | async-start | bytes 4866048 | tf_op jit(solution)/shard_map/all_gather | solution.py:113
  9.4 250.9 %all-gather.11.cloned.1.call-start = ((), (), s32[]{:S(2)}) async-start(), calls=%async_computation.3 | async-start | bytes 4866048 | tf_op jit(solution)/shard_map/all_gather | solution.py:114
  10.0 868.6 %all-reduce.9.cloned.1.call-start = ((), (), s32[]{:S(2)}) async-start(), calls=%async_computation.4 | async-start | bytes 56623104
  62.6 74.6 %copy-start.6 = (bf16[1024,768]{1,0:T(8,128)(2,1)S(1)}, bf16[1024,768]{1,0:T(8,128)(2,1)}, u32[]{:S(2)}) copy-start(bf16[1024,768]{1,0:T(8,128)(2,1)} %param.14) | copy-start | bytes 4718596
  160.1 5.7 copy-start.32
  165.8 24.9 %copy-start.29 = (f32[768]{0:T(1024)S(1)}, f32[768]{0:T(1024)}, u32[]{:S(2)}) copy-start(f32[768]{0:T(1024)} %get-tuple-element.175) | copy-start | bytes 9220
  189.6 5.1 copy-start.11
  195.1 8.3 copy-start.13
  195.1 8.3 copy-start.17
  195.1 8.3 copy-start.26
  195.1 8.3 copy-start.27
  241.3 28.6 %copy-start.28 = (f32[768]{0:T(1024)S(1)}, f32[768]{0:T(1024)}, u32[]{:S(2)}) copy-start(f32[768]{0:T(1024)} %get-tuple-element.172) | copy-start | bytes 9220
  269.9 9.4 %copy-start.16 = (f32[768]{0:T(1024)S(1)}, f32[768]{0:T(1024)}, u32[]{:S(2)}) copy-start(f32[768]{0:T(1024)} %get-tuple-element.170) | copy-start | bytes 9220
  285.9 7.6 copy-start.8
  312.7 10.4 %copy-start.35 = (bf16[1024,3072]{1,0:T(8,128)(2,1)S(1)}, bf16[1024,3072]{1,0:T(8,128)(2,1)}, u32[]{:S(2)}) copy-start(bf16[1024,3072]{1,0:T(8,128)(2,1)} %get-tuple-element.185) | copy-start | bytes 18874372
  323.1 7.7 copy-start.14
  331.6 3.6 copy-start.3
  331.7 3.6 copy-start.22
  413.5 6.8 copy-start.7
  436.7 8.1 copy-start.5
  460.0 5.8 copy-start.15
  460.0 5.9 copy-start.21
  460.0 5.9 copy-start.31
  460.0 5.9 copy-start.30
  460.0 5.9 copy-start.25
  460.1 6.0 copy-start.20
  460.1 6.0 copy-start.24
  460.1 6.0 copy-start.19
  460.1 425.1 %copy-start.1 = (bf16[2,128,768]{2,1,0:T(8,128)(2,1)S(1)}, bf16[2,128,768]{2,1,0:T(8,128)(2,1)}, u32[]{:S(2)}) copy-start(bf16[2,128,768]{2,1,0:T(8,128)(2,1)} %param.23) | copy-start | bytes 1179652
  (11 other events, 25.6 us)
Sparse Core Ops, SparseCore 0:
  10.9 56.7 all-gather.6
  70.6 58.9 all-gather.4
  132.5 62.4 all-gather.8
  197.8 62.4 all-gather.10
  446.5 432.0 all-reduce.8
where the time goes:
time: 900 us; the launch traced here: 892 us
  waiting for transfers between devices  455 us (51%)
  matrix products  170 us (19%)
  local copies, waits for them, and re-layouts  134 us (15%)
  blocking collectives  83.9 us (9%)
  other arithmetic  33.4 us (4%)
  between operations  14.8 us (2%)
    unnamed x6, waiting for transfers between devices  373 us
    unnamed x2, blocking collectives  83.9 us
    all_gather x1, waiting for transfers between devices, on_device(): lax.all_gather(qkv_weight, ('dp', 'inner'), axis=0, tiled=True)  58.6 us
    dot_general x4, matrix products, matmul(): return jnp.dot(left, right, preferred_element_type=jnp.float32)  58.2 us
    dot_general x4, matrix products, contract_cols(): lax.dot_general(left, right, (((1,), (1,)), ((), ())), preferred_element_...  40.2 us
    unnamed x95, local copies, waits for them, and re-layouts  31.3 us
    dot_general x4, matrix products, contracted_row_axes(): lax.dot_general(left, right, (((0,), (0,)), ((), ())), preferred_element_...  26.5 us
    all_gather x1, waiting for transfers between devices, on_device(): lax.all_gather(down_weight, ('dp', 'inner'), axis=0, tiled=True)  19 us
  transfers between devices with their start and end apart: 5, of which 4 were waited for; matrix products, arithmetic and copies ran while one was open for 16% of the time, Pallas kernels for 0%

commit v1 on v0

--- a/solution.py
+++ b/solution.py
@@ -3,7 +3,298 @@
 import jax
 import jax.numpy as jnp
 from jax import lax
+from jax.experimental import pallas as pl
+from jax.experimental.pallas import tpu as pltpu
 from jax.sharding import PartitionSpec as P
+
+bf = jnp.bfloat16
+f32 = jnp.float32
+MESH = pl.DeviceIdType.MESH
+NU = 12
+C, X, Y, Z0, Z1 = range(5)
+A = slice(None)
+gather_order = (
+    "0z1", "1z1", "2z1", "11z1", "8s0", "6s0", "10s0", "5s0", "9s0", "7s0", "0z0", "1z0", "3z1",
+    "0B1", "0A1", "2z0", "8z1", "4z1", "1B1", "1A1", "0B2", "0A2", "2B1", "11z0", "1A2", "3z0",
+    "2A1", "1B2", "4z0", "7z1", "6z1", "0C", "2A2", "4B1", "2B2", "3B1", "7z0", "11B1", "3A1",
+    "1C", "11A1", "8z0", "2C", "4A1", "3A2", "6z0", "5z1", "9z1", "3B2", "7s3", "4A2", "10z1",
+    "4B2", "8s3", "5z0", "3C", "9z0", "6s3", "7C", "5s3", "4C", "10z0", "9s3", "8C", "11B2",
+    "10s3", "11A2", "5C", "6C", "9C", "10C", "11C",
+)
+scatter_order = (
+    "0C", "1C", "0s3", "3C", "1s3", "4C", "2C", "4s3", "7C", "3s3", "5C", "7A2", "8C", "6C", "2s3",
+    "0z0", "8B2", "7B2", "5s3", "1z0", "4z0", "8A2", "8B1", "3z0", "9C", "6A2", "0z1", "10C",
+    "11C", "6B2", "11A2", "4z1", "2z0", "11B2", "1z1", "8A1", "3z1", "6B1", "6A1", "5z0", "11B1",
+    "7A1", "11A1", "9A2", "9B2", "8z0", "2z1", "10B2", "6z0", "7B1", "8z1", "11z0", "5z1", "10A2",
+    "7z0", "3s0", "9B1", "11z1", "9A1", "6z1", "10A1", "10B1", "7z1", "4s0", "2s0", "9z0", "5s0",
+    "1s0", "10z0", "0s0", "9z1", "10z1",
+)
+
+scatter_units = (4, 5, 6, 7, 8, 9, 10, 11, 3, 1, 0, 2)
+gather_types = ("ab",) * 5 + ("e", "f") * 3 + ("ab",)
+scatter_types = ("f", "e") * 3 + ("ab",) * 6
+
+
+def parse(order):
+    digits = [2 if o[1].isdigit() else 1 for o in order]
+    return [(int(o[:d]), o[d:]) for o, d in zip(order, digits)]
+
+
+class Place:
+    def __init__(self, dp_size, inner_size):
+        n=dp_size*inner_size
+        self.nsub=n//32
+        self.inner=inner_size
+        lin=lax.axis_index("dp")*inner_size+lax.axis_index("inner")
+        self.sub=lin%self.nsub
+        self.g=lin//self.nsub
+        self.bit=[(self.g//(2**b))%2 for b in range(5)]
+        self.c,self.x,self.y,self.z0,self.z1=self.bit
+    def partner(self,b):
+        g=self.g+2**b-2*(2**b)*self.bit[b]
+        lin=g*self.nsub+self.sub
+        return (lin//self.inner, lin%self.inner)
+
+def remote(src,dst,ss,rs,dev):
+    return pltpu.make_async_remote_copy(src_ref=src,dst_ref=dst,send_sem=ss,recv_sem=rs,device_id=dev,device_id_type=MESH)
+
+class Gather:
+    def __init__(self,pos,W,ss,rs,types):
+        self.p=pos; self.W=W; self.ss=ss; self.rs=rs; self.types=types
+        self.cols=pl.ds(pl.multiple_of(384*pos.c,128),384)
+        z1,z0,y,x=pos.z1,pos.z0,pos.y,pos.x
+        head=[("z1",(),Z1,(z1,z0,y,x)),("z0",("z1",),Z0,(A,z0,y,x))]
+        whole=(A,A,A,A)
+        self.legs={
+            "ab":head+[("A1",("z0",),Y,(0,A,y,x)),("B1",("z0",),X,(1,A,y,x)),
+                       ("A2",("A1",),X,(0,A,A,x)),("B2",("B1",),Y,(1,A,y,A)),("C",("A2","B2"),C,whole)],
+            "e":[("s0",(),X,(z1,z0,y,x)),("z1",("s0",),Z1,(z1,z0,y,A)),("z0",("z1",),Z0,(A,z0,y,A)),("s3",("z0",),Y,(A,A,y,A)),("C",("s3",),C,whole)],
+            "f":[("s0",(),Y,(z1,z0,y,x)),("z1",("s0",),Z1,(z1,z0,A,x)),("z0",("z1",),Z0,(A,z0,A,x)),("s3",("z0",),X,(A,A,A,x)),("C",("s3",),C,whole)],
+        }
+        self.got=set(); self.sent=[]
+    def copy(self,m,n):
+        L=self.legs[self.types[m]]
+        k=[l[0] for l in L].index(n)
+        _,_,b,idx=L[k]
+        r=self.W.at[(m,)+idx+(A,self.cols)]
+        return remote(r,r,self.ss.at[m,k],self.rs.at[m,k],self.p.partner(b)), L[k][1]
+    def arrive(self,m,n):
+        if (m,n) in self.got: return
+        self.got.add((m,n)); self.copy(m,n)[0].wait_recv()
+    def op(self,m,n):
+        c,deps=self.copy(m,n)
+        for d in deps: self.arrive(m,d)
+        c.start(); self.sent.append((m,n))
+    def drain(self):
+        for m,n in self.sent: self.copy(m,n)[0].wait_send()
+
+class Scatter:
+    def __init__(self,pos,P,R,ss,rs,rdy,types,order):
+        self.p=pos; self.P=P; self.R=R; self.ss=ss; self.rs=rs; self.rdy=rdy; self.types=types
+        c,x,y,z0,z1=pos.c,pos.x,pos.y,pos.z0,pos.z1
+        self.legs={
+            "ab":[("A2",("C",),X,(0,A,A,1-x),(0,A,A,1-x),(0,A,A,x),(0,A,A,x)),
+                  ("B2",("C",),Y,(1,A,1-y,A),(1,A,1-y,A),(1,A,y,A),(1,A,y,A)),
+                  ("A1",("A2",),Y,(0,A,1-y,x),(0,A,1-y,1-x),(0,A,y,x),(0,A,y,1-x)),
+                  ("B1",("B2",),X,(1,A,y,1-x),(1,A,1-y,1-x),(1,A,y,x),(1,A,1-y,x)),
+                  ("z0",("A1","B1"),Z0,(A,1-z0,y,x),(A,1-z0,1-y,1-x),(A,z0,y,x),(A,z0,1-y,1-x)),
+                  ("z1",("z0",),Z1,(1-z1,z0,y,x),(1-z1,1-z0,1-y,1-x),(z1,z0,y,x),(z1,1-z0,1-y,1-x))],
+            "e":[("s3",("C",),Y,(A,A,1-y,A),(A,A,1-y,A),(A,A,y,A),(A,A,y,A)),
+                 ("z0",("s3",),Z0,(A,1-z0,y,A),(A,1-z0,1-y,A),(A,z0,y,A),(A,z0,1-y,A)),
+                 ("z1",("z0",),Z1,(1-z1,z0,y,A),(1-z1,1-z0,1-y,A),(z1,z0,y,A),(z1,1-z0,1-y,A)),
+                 ("s0",("z1",),X,(z1,z0,y,1-x),(1-z1,1-z0,1-y,1-x),(z1,z0,y,x),(1-z1,1-z0,1-y,x))],
+            "f":[("s3",("C",),X,(A,A,A,1-x),(A,A,A,1-x),(A,A,A,x),(A,A,A,x)),
+                 ("z0",("s3",),Z0,(A,1-z0,A,x),(A,1-z0,A,1-x),(A,z0,A,x),(A,z0,A,1-x)),
+                 ("z1",("z0",),Z1,(1-z1,z0,A,x),(1-z1,1-z0,A,1-x),(z1,z0,A,x),(z1,1-z0,A,1-x)),
+                 ("s0",("z1",),Y,(z1,z0,1-y,x),(1-z1,1-z0,1-y,1-x),(z1,z0,y,x),(1-z1,1-z0,y,1-x))],
+        }
+        self.got=set(); self.sent=[]
+        self.turn={}
+        for m,n in order:
+            for d in self.leg(m,n)[1]:
+                if d=="C" and m not in self.turn: self.turn[m]=len(self.turn)
+        self.heard={b:0 for b in (X,Y,Z0,Z1)}
+    def leg(self,m,n):
+        if n=="C": return ("C",(),C)
+        return [l for l in self.legs[self.types[m]] if l[0]==n][0]
+    def copy(self,m,n):
+        c=self.p.c
+        if n=="C":
+            return remote(self.P.at[m,1-c],self.R.at[m],self.ss.at[m,0],self.rs.at[m,0],self.p.partner(C))
+        L=self.legs[self.types[m]]
+        k=[l[0] for l in L].index(n)
+        _,_,b,snd,lnd,_,_=L[k]
+        return remote(self.P.at[(m,c)+snd],self.P.at[(m,1-c)+lnd],self.ss.at[m,k+1],self.rs.at[m,k+1],self.p.partner(b))
+    def add(self,m,n):
+        if (m,n) in self.got: return
+        self.got.add((m,n)); c=self.p.c
+        d=self.copy(m,n)
+        if n=="C":
+            d.wait_send(); self.sent.remove((m,n))
+            for b in (X,Y,Z0,Z1):
+                pl.semaphore_signal(self.rdy.at[b-1],inc=1,device_id=self.p.partner(b),device_id_type=MESH)
+            d.wait_recv()
+            self.P[m,c]=self.P[m,c]+self.R[m]
+            return
+        d.wait_recv()
+        _,_,_,_,_,own,got=self.leg(m,n)
+        i=(m,c)+own
+        self.P[i]=self.P[i]+self.P[(m,1-c)+got]
+    def op(self,m,n):
+        L=self.leg(m,n)
+        for d in L[1]: self.add(m,d)
+        b=L[2]
+        if b!=C:
+            need=self.turn[m]+1-self.heard[b]
+            if need>0:
+                pl.semaphore_wait(self.rdy.at[b-1],need); self.heard[b]+=need
+        self.copy(m,n).start(); self.sent.append((m,n))
+    def last(self,m):
+        n=self.legs[self.types[m]][-1][0]
+        self.copy(m,n).wait_recv()
+        c=self.p.c
+        _,_,_,_,_,own,got=self.leg(m,n)
+        v=self.P[(m,c)+own].astype(f32)+self.P[(m,1-c)+got].astype(f32)
+        top=v[0:8]; bot=v[8:16]
+        return jnp.concatenate([jnp.concatenate([top[:,384*k:384*k+384],bot[:,384*k:384*k+384]],1) for k in range(3)],0)
+    def drain(self):
+        for m,n in self.sent: self.copy(m,n).wait_send()
+        for b in (X,Y,Z0,Z1):
+            left=NU-self.heard[b]
+            if left>0: pl.semaphore_wait(self.rdy.at[b-1],left)
+def enter(pos):
+    b=pltpu.get_barrier_semaphore()
+    for k in range(5):
+        pl.semaphore_signal(b,inc=1,device_id=pos.partner(k),device_id_type=MESH)
+    pl.semaphore_wait(b,5)
+
+
+def gather_kernel(dp_size, inner_size, sh, w2, wout, W, SHR, ss, rs, fs, ls):
+    pos = Place(dp_size, inner_size)
+    enter(pos)
+    c = pos.c
+    G = Gather(pos, W, ss, rs, gather_types)
+    oc = pl.ds(pl.multiple_of(384 * (1 - c), 128), 384)
+    cp = remote(sh.at[:, :, oc], SHR, fs.at[0], fs.at[1], pos.partner(C))
+    cp.start()
+    chip = (pos.z1, pos.z0, pos.y, pos.x)
+    cp2 = [
+        remote(
+            w2.at[j, :, oc],
+            W.at[(8 + 2 * c + j,) + chip + (A, oc)],
+            fs.at[2 + 2 * j],
+            fs.at[3 + 2 * j],
+            pos.partner(C),
+        )
+        for j in range(2)
+    ]
+    for q in cp2:
+        q.start()
+    for j in range(2):
+        W[(8 + 2 * c + j,) + chip + (A, G.cols)] = w2[j, :, G.cols]
+    cp.wait_recv()
+    for u in range(8):
+        own = sh[u, :, G.cols]
+        oth = SHR[u]
+        lo = jnp.where(c == 0, own, oth)
+        hi = jnp.where(c == 0, oth, own)
+        W[(u,) + chip + (A, G.cols)] = jnp.concatenate([lo, hi], 0).astype(bf)
+    for q in cp2:
+        q.wait_recv()
+    for m, n in parse(gather_order):
+        G.op(m, n)
+    for m in range(NU):
+        G.arrive(m, "C")
+    cp.wait_send()
+    for q in cp2:
+        q.wait_send()
+    G.drain()
+    o = pltpu.make_async_copy(W, wout, ls)
+    o.start()
+    o.wait()
+
+
+def scatter_kernel(dp_size, inner_size, p_in, gw, P, R, ss, rs, rdy, ls):
+    pos = Place(dp_size, inner_size)
+    o = pltpu.make_async_copy(p_in, P, ls)
+    o.start()
+    enter(pos)
+    o.wait()
+    S = Scatter(pos, P, R, ss, rs, rdy, scatter_types, parse(scatter_order))
+    for m, n in parse(scatter_order):
+        S.op(m, n)
+    for m in range(NU):
+        gw[m] = S.last(m)
+    S.drain()
+
+
+VM = pl.BlockSpec(memory_space=pltpu.VMEM)
+ANY = pl.BlockSpec(memory_space=pl.ANY)
+
+
+def gather_call(sizes, sh, w2):
+    return pl.pallas_call(
+        partial(gather_kernel, *sizes),
+        out_shape=jax.ShapeDtypeStruct((NU, 2, 2, 2, 2, 48, 768), bf),
+        in_specs=[VM] * 2,
+        out_specs=ANY,
+        scratch_shapes=[
+            pltpu.VMEM((NU, 2, 2, 2, 2, 48, 768), bf),
+            pltpu.VMEM((8, 24, 384), f32),
+            pltpu.SemaphoreType.DMA((NU, 7)),
+            pltpu.SemaphoreType.DMA((NU, 7)),
+            pltpu.SemaphoreType.DMA((6,)),
+            pltpu.SemaphoreType.DMA,
+        ],
+        compiler_params=pltpu.CompilerParams(
+            collective_id=0, has_side_effects=True, vmem_limit_bytes=32 * 2**20
+        ),
+    )(sh, w2)
+
+
+def scatter_call(sizes, p):
+    return pl.pallas_call(
+        partial(scatter_kernel, *sizes),
+        out_shape=jax.ShapeDtypeStruct((NU, 24, 768), f32),
+        in_specs=[ANY],
+        out_specs=VM,
+        scratch_shapes=[
+            pltpu.VMEM((NU, 2, 2, 2, 2, 2, 16, 1152), bf),
+            pltpu.VMEM((NU, 2, 2, 2, 2, 16, 1152), bf),
+            pltpu.SemaphoreType.DMA((NU, 7)),
+            pltpu.SemaphoreType.DMA((NU, 7)),
+            pltpu.SemaphoreType.REGULAR((4,)),
+            pltpu.SemaphoreType.DMA,
+        ],
+        compiler_params=pltpu.CompilerParams(
+            collective_id=1, has_side_effects=True, vmem_limit_bytes=40 * 2**20
+        ),
+    )(p)
+
+
+def groups_of(sizes):
+    sub = sizes[0] * sizes[1] // 32
+    return [[sub * i + j for j in range(sub)] for i in range(32)]
+
+
+def pre(sizes, flat):
+    if sizes[0] * sizes[1] == 32:
+        return flat
+    return lax.all_gather(flat, ("dp", "inner"), axis_index_groups=groups_of(sizes), tiled=True)
+
+
+def post(sizes, flat):
+    if sizes[0] * sizes[1] == 32:
+        return flat
+    return lax.psum_scatter(
+        flat, ("dp", "inner"), axis_index_groups=groups_of(sizes), scatter_dimension=0, tiled=True
+    )
+
+
+def wire(unit):
+    v = unit.reshape(16, 2, 3, 8, 2, 384).transpose(1, 0, 4, 3, 2, 5)
+    return v.reshape(2, 2, 2, 2, 2, 16, 1152).astype(bf)
+
 
 D = 768
 H = 12
@@ -93,6 +384,7 @@
 
 
 def on_device(
+    sizes,
     inputs,
     qkv_weight,
     out_weight,
@@ -104,22 +396,20 @@
     positions,
     grad_values,
 ):
-    attn_parts = (
-        lax.all_gather(qkv_weight, ("dp", "inner"), axis=0, tiled=True),
-        lax.all_gather(out_weight, ("dp", "inner"), axis=0, tiled=True),
-        lax.all_gather(vectors, ("dp", "inner"), axis=0, tiled=True),
-    )
-    ffn_parts = (
-        lax.all_gather(up_weight, ("dp", "inner"), axis=0, tiled=True),
-        lax.all_gather(down_weight, ("dp", "inner"), axis=0, tiled=True),
-    )
-    qkv_matrix = attn_parts[0].reshape(D, 3 * D)
-    output_projection = attn_parts[1].reshape(D, D)
+    fq, fo, fu, fd = [pre(sizes, w) for w in (qkv_weight, out_weight, up_weight, down_weight)]
+    fq = fq.reshape(24, 3, 768)
+    fq = jnp.stack([fq[:, 1], fq[:, 2], fq[:, 0]])
+    fu = fu.reshape(24, 4, 768).transpose(1, 0, 2)
+    sh = jnp.concatenate([fq, fo.reshape(1, 24, 768), fu], 0).astype(f32)
+    units = gather_call(sizes, sh, fd.reshape(2, 48, 768)).reshape(12, 768, 768)
+    qkv_matrix = jnp.concatenate([units[2], units[0], units[1]], 1)
+    output_projection = units[3]
+    up_matrix = jnp.concatenate([units[4 + i] for i in range(4)], 1)
+    down_matrix = units[8:].reshape(4, 16, 48, 768).transpose(1, 0, 2, 3).reshape(FF, D)
+    vec = lax.all_gather(vectors, ("dp", "inner"), axis=0, tiled=True)
     q_bias, v_bias, out_bias, gain_one, shift_one, up_bias, down_bias, gain_two, shift_two = (
-        split_vectors(attn_parts[2].astype(jnp.float32))
-    )
-    up_matrix = ffn_parts[0].reshape(D, FF)
-    down_matrix = ffn_parts[1].reshape(FF, D)
+        split_vectors(vec.astype(jnp.float32))
+    )
     groups = inputs.shape[0] // SEQ_LEN
     qkv_bias = jnp.concatenate([q_bias, jnp.zeros_like(q_bias), v_bias])
     joined = (matmul(inputs, qkv_matrix) + qkv_bias).astype(jnp.bfloat16)
@@ -149,12 +439,6 @@
         preferred_element_type=jnp.float32,
     ).reshape(-1, D)
     d_two, gain_two_grad, shift_two_grad = second_pull(cotangent)
-    ffn_back = (
-        lax.all_gather(up_weight, ("dp", "inner"), axis=0, tiled=True),
-        lax.all_gather(down_weight, ("dp", "inner"), axis=0, tiled=True),
-    )
-    up_matrix = ffn_back[0].reshape(D, FF)
-    down_matrix = ffn_back[1].reshape(FF, D)
     ffn_grad = d_two.astype(jnp.bfloat16)
     down_grad = contracted_row_axes(active_low, ffn_grad)
     down_bias_grad = jnp.sum(ffn_grad.astype(jnp.float32), 0)
@@ -163,19 +447,7 @@
     up_weight_gradient = contracted_row_axes(normed_low, pre_grad)
     up_bias_grad = jnp.sum(pre_grad.astype(jnp.float32), 0)
     d_normed = d_two + contract_cols(pre_grad, up_matrix)
-    ffn_sums = (
-        lax.psum_scatter(
-            up_weight_gradient.reshape(-1), ("dp", "inner"), scatter_dimension=0, tiled=True
-        ),
-        lax.psum_scatter(down_grad.reshape(-1), ("dp", "inner"), scatter_dimension=0, tiled=True),
-    )
     d_one, gain_one_grad, shift_one_grad = first_pull(d_normed)
-    attn_back = (
-        lax.all_gather(qkv_weight, ("dp", "inner"), axis=0, tiled=True),
-        lax.all_gather(out_weight, ("dp", "inner"), axis=0, tiled=True),
-    )
-    qkv_matrix = attn_back[0].reshape(D, 3 * D)
-    output_projection = attn_back[1].reshape(D, D)
     attn_grad = d_one.astype(jnp.bfloat16)
     out_grad = contracted_row_axes(context_low, attn_grad)
     out_bias_grad = jnp.sum(attn_grad.astype(jnp.float32), 0)
@@ -202,19 +474,24 @@
             shift_two_grad,
         ]
     )
-    attn_sums = (
-        lax.psum_scatter(qkv_grad.reshape(-1), ("dp", "inner"), scatter_dimension=0, tiled=True),
-        lax.psum_scatter(out_grad.reshape(-1), ("dp", "inner"), scatter_dimension=0, tiled=True),
-        lax.psum_scatter(vector_grad, ("dp", "inner"), scatter_dimension=0, tiled=True),
-    )
+    cols = [qkv_grad[:, 768:1536], qkv_grad[:, 1536:], qkv_grad[:, :768], out_grad]
+    cols += [up_weight_gradient[:, 768 * i : 768 * i + 768] for i in range(4)]
+    dg = down_grad.reshape(32, 4, 24, 768)
+    cols += [dg[:, i].reshape(768, 768) for i in range(4)]
+    turned = [cols[i] for i in scatter_units]
+    gw = scatter_call(sizes, jnp.stack([wire(u) for u in turned]))
+    back = [gw[scatter_units.index(u)] for u in range(12)]
+    g_qkv = jnp.concatenate([back[2], back[0], back[1]], 1)
+    g_up = jnp.concatenate(back[4:8], 1)
+    g_down = jnp.concatenate(back[8:], 0)
     return (
         layer_out.astype(jnp.bfloat16),
         input_grad,
-        attn_sums[0],
-        attn_sums[1],
-        ffn_sums[0],
-        ffn_sums[1],
-        attn_sums[2],
+        post(sizes, g_qkv.reshape(-1)),
+        post(sizes, back[3].reshape(-1)),
+        post(sizes, g_up.reshape(-1)),
+        post(sizes, g_down.reshape(-1)),
+        lax.psum_scatter(vector_grad, ("dp", "inner"), scatter_dimension=0, tiled=True),
     )
 
 
@@ -232,7 +509,7 @@
         P(("dp", "inner"), None, None),
     )
     return jax.shard_map(
-        on_device,
+        partial(on_device, (mesh.shape["dp"], mesh.shape["inner"])),
         mesh=mesh,
         in_specs=placed,
         out_specs=(

time: 900 us -> 565 us (0.63)
  waiting for transfers between devices: 455 us -> 0 us
  Pallas kernels: 0 us -> 141 us
  between operations: 14.8 us -> 1.91 us
    unnamed x6 -> x0, waiting for transfers between devices: 373 us -> none
    pallas_call x0 -> x2, Pallas kernels: none -> 141 us  [the longest x1 71.7 us: gather_call(): pl.pallas_call(partial(gather_kernel, *sizes), out_shape=jax.ShapeDtypeSt...]
    all_gather x4 -> x0, waiting for transfers between devices: 82.6 us -> none  [the longest x1 58.6 us: on_device(): lax.all_gather(qkv_weight, ('dp', 'inner'), axis=0, tiled=True)]
    reshape x7, local copies, waits for them, and re-layouts: 49.2 us -> 8.07 us  [the longest x1 2.84 us: on_device(): units[8:].reshape(4, 16, 48, 768).transpose(1, 0, 2, 3).reshape(FF, D)]
    convert_element_type x1 -> x19, local copies, waits for them, and re-layouts: 6.61 us -> 40.6 us  [wire(): return v.reshape(2, 2, 2, 2, 2, 16, 1152).astype(bf)]
    slice x0 -> x8, local copies, waits for them, and re-layouts: none -> 12 us  [the longest x2 5.6 us: on_device(): qkv_grad[:, :768]]
    unnamed x95 -> x157, local copies, waits for them, and re-layouts: 31.3 us -> 21.8 us
  transfers between devices with their start and end apart: 5 -> 0, of which waited for: 4 -> 0; matrix products, arithmetic and copies ran while one was open for 16% -> 0% of each run, Pallas kernels for 0% -> 0%
where the time goes in v1:
time: 565 us; the launch traced here: 557 us
  matrix products  167 us (30%)
  Pallas kernels  141 us (25%)
  local copies, waits for them, and re-layouts  128 us (23%)
  blocking collectives  81 us (14%)
  other arithmetic  37.7 us (7%)
    unnamed x2, blocking collectives  81 us
    pallas_call x1, Pallas kernels, gather_call(): pl.pallas_call(partial(gather_kernel, *sizes), out_shape=jax.ShapeDtypeSt...  71.7 us
    pallas_call x1, Pallas kernels, scatter_call(): pl.pallas_call(partial(scatter_kernel, *sizes), out_shape=jax.ShapeDtypeS...  69.2 us
    dot_general x4, matrix products, matmul(): return jnp.dot(left, right, preferred_element_type=jnp.float32)  57.1 us
    convert_element_type x19, local copies, waits for them, and re-layouts, wire(): return v.reshape(2, 2, 2, 2, 2, 16, 1152).astype(bf)  40.6 us
    dot_general x4, matrix products, contract_cols(): lax.dot_general(left, right, (((1,), (1,)), ((), ())), preferred_element_...  38.4 us
    dot_general x4, matrix products, contracted_row_axes(): lax.dot_general(left, right, (((0,), (0,)), ((), ())), preferred_element_...  25.3 us
    unnamed x157, local copies, waits for them, and re-layouts  21.8 us

profile of v1, /device:TPU:0, one launch (start us, length us, event | category | flops | bytes accessed | tf_op | source)
XLA Modules:
  0.0 557.1 jit_solution(7907028312245469504)
XLA Ops:
  3.1 42.2 %all-reduce = bf16[9216]{0:T(1024)(128)(2,1)S(1)} all-reduce(bf16[9216]{0:T(1024)(128)(2,1)S(1)} %dynamic-update-slice), channel_id=1, replica_groups=mesh['dp'=8,'inner'=4] {'dp','inner'}, use_global_device_ids=true, to_apply=%add | all-reduce | flops 9216 | bytes 36864
  55.2 3.6 copy.164
  58.7 71.7 %shard_map.153 = bf16[12,2,2,2,2,48,768]{6,5,4,3,2,1,0:T(8,128)(2,1)S(1)} custom-call(f32[8,24,768]{2,1,0:T(8,128)S(1)} %convert_element_type.284.sh, bf16[2,48,768]{2,1,0:T(8,128)(2,1)S(1)} %reshape.383.w2), custom_call_target="tpu_custom_call" | custom-call | tf_op jit(solution)/shard_map/pallas_call | solution.py:236
  136.7 6.4 %fusion.34 = bf16[1024,2304]{0,1:T(8,128)(2,1)} fusion(bf16[1024,768]{1,0:T(8,128)(2,1)S(1)} %copy-done.21, f32[2304]{0:T(1024)S(1)} %pad_maximum_fusion.9, bf16[768,768]{1,0:T(8,128)(2,1)S(1)} %bitcast.292, bf16[768,768]{1,0:T(8,128)(2,1)S(1)} %bitcast.294, bf16[768,768]{1,0:T(8,128)(2,1)S(1)} %bitcast.296), kind=kOutput, calls=%fused_computation.69 | convolution fusion | flops 3639214080 | bytes 9839616 | tf_op jit(solution)/shard_map/dot_general | solution.py:326
  143.1 8.8 %reshape.384 = bf16[2,512,3,12,64]{1,0,4,3,2:T(2,128)(2,1)} reshape(bf16[1024,2304]{0,1:T(8,128)(2,1)} %fusion.34) | data formatting | bytes 9437184 | tf_op jit(solution)/shard_map/reshape | solution.py:416
  151.9 5.6 copy.126
  157.5 24.6 %while.22 = (s32[]{:T(128)}, bf16[2,512,768]{2,1,0:T(8,128)(2,1)}, f32[2,12,512,1]{2,1,3,0:T(8,128)S(1)}, bf16[2,512,3,12,64]{1,4,3,2,0:T(8,128)(2,1)}, pred[2,512]{1,0:T(4,128)(4,1)S(1)}, /*index=5*/s32[]{:T(128)}) while((s32[]{:T(128)}, bf16[2,512,768]{2,1,0:T(8,128)(2,1)}, f32[2,12,512,1]{2,1,3,0:T(8,128)S(1)}, ...), condition=%wide.region_3.4_spmd, body=%wide.region_0.3_spmd.sunk | while | flops 843048960 | bytes 48999004 | solution.py:418
  165.5 3.3 fusion.97
  184.8 4.0 fusion.60
  189.2 39.1 %multiply_convert_fusion.3 = (bf16[1024,3072]{1,0:T(8,128)(2,1)}, f32[1024,3072]{1,0:T(8,128)}, f32[1024,3072]{1,0:T(8,128)}) fusion(f32[3072]{0:T(1024)S(1)} %copy-done.53, bf16[768,768]{1,0:T(8,128)(2,1)S(1)} %bitcast.302, bf16[768,768]{1,0:T(8,128)(2,1)S(1)} %bitcast.304, bf16[768,768]{1,0:T(8,128)(2,1)S(1)} %bitcast.306, ...), kind=kOutput, calls=%fused_computation.50 | convolution fusion | flops 5062262784 | bytes 39348224 | tf_op jit(solution)/shard_map/dot_general | solution.py:326
  228.5 7.6 %fusion.61 = (f32[1024]{0:T(1024)S(1)}, f32[1024,768]{0,1:T(8,128)S(1)}) fusion(f32[768]{0:T(1024)S(1)} %copy-done.56, bf16[1024,3072]{1,0:T(8,128)(2,1)} %get-tuple-element.177, bf16[3072,768]{1,0:T(8,128)(2,1)S(1)} %bitcast.265, f32[768]{0:T(1024)S(1)} %copy-done.55, f32[768]{0:T(1024)S(1)} %copy-done.45, f32[1024]{0:T(1024)S(1)} %fusion.44, ...), kind=kOutput, calls=%fused_computation.173 | convolution fusion | flops 4837342208 | bytes 17323008 | tf_op jit(solution)/shard_map/dot_general | solution.py:326
  248.1 17.6 %convert_reduce_fusion = (f32[3072]{0:T(1024)}, bf16[1024,3072]{1,0:T(8,128)(2,1)}) fusion(f32[1024,3072]{1,0:T(8,128)} %get-tuple-element.178, bf16[1024,768]{0,1:T(8,128)(2,1)S(1)} %get-tuple-element.170, bf16[3072,768]{1,0:T(8,128)(2,1)} %bitcast.262, f32[1024,3072]{1,0:T(8,128)} %get-tuple-element.228, f32[3072]{0:T(1024)S(1)} %copy-done.53), kind=kOutput, calls=%fused_computation.48 | convolution fusion | flops 4885312512 | bytes 37773312 | tf_op jit(solution)/shard_map/dot_general | solution.py:336
  265.7 8.9 %convolution_convert_fusion = bf16[3072,768]{1,0:T(8,128)(2,1)S(1)} fusion(bf16[1024,3072]{1,0:T(8,128)(2,1)} %get-tuple-element.177, bf16[1024,768]{0,1:T(8,128)(2,1)S(1)} %get-tuple-element.170), kind=kOutput, calls=%fused_computation.66 | convolution fusion | flops 4834197504 | bytes 12582912 | tf_op jit(solution)/shard_map/dot_general | solution.py:330
  274.7 10.9 %multiply_reduce_fusion.2 = (f32[768]{0:T(1024)}, f32[1024]{0:T(1024)S(1)}, f32[768]{0:T(1024)}, f32[1024,768]{0,1:T(8,128)}) fusion(f32[1024,768]{0,1:T(8,128)S(1)} %get-tuple-element.227, f32[1024]{0:T(1024)S(1)} %fusion.44, f32[1024]{0:T(1024)S(1)} %broadcast_multiply_fusion.1, f32[768]{0:T(1024)S(1)} %copy-done.45, ...), kind=kOutput, calls=%fused_computation.77 | convolution fusion | flops 4858573824 | bytes 20472832 | tf_op jit(solution)/shard_map/dot_general | solution.py:336
  288.9 3.8 fusion.52
  292.8 9.5 %convolution_convert_fusion.1 = bf16[768,3072]{1,0:T(8,128)(2,1)S(1)} fusion(bf16[1024,3072]{1,0:T(8,128)(2,1)} %get-tuple-element.233, f32[1024,768]{0,1:T(8,128)S(1)} %copy-done.7, f32[768]{0:T(1024)S(1)} %copy-done.55, f32[768]{0:T(1024)S(1)} %copy-done.45, f32[1024]{0:T(1024)S(1)} %fusion.44, f32[1024]{0:T(1024)S(1)} %broadcast_multiply_fusion.1), kind=kOutput, calls=%fused_computation.67 | convolution fusion | flops 4838129664 | bytes 14170112 | tf_op jit(solution)/shard_map/dot_general | solution.py:330
  307.1 3.6 convert_element_type.316
  313.1 3.8 convert_element_type.313
  319.3 3.6 convert_element_type.310
  332.8 52.9 %while.23 = (s32[]{:T(128)}, bf16[2,512,2304]{1,2,0:T(8,128)(2,1)}, bf16[2,512,3,12,64]{1,4,3,2,0:T(8,128)(2,1)}, pred[2,512]{1,0:T(4,128)(4,1)S(1)}, f32[2,12,5...) while((s32[]{:T(128)}, bf16[2,512,2304]{1,2,0:T(8,128)(2,1)}, ...), condition=%wide.region_14.15_spmd, body=%wide.region_12.14_spmd.sunk | while | flops 2064771072 | bytes 116583024 | solution.py:459
  340.0 7.3 %multiply_reduce_fusion.8 = (f32[12,512]{1,0:T(8,128)S(1)}, f32[12,512,512]{1,2,0:T(8,128)}) fusion(f32[12,512,512]{1,2,0:T(8,128)S(1)} %fusion.102, f32[12,512]{1,0:T(8,128)S(1)} %dynamic-slice_bitcast_fusion.8, pred[512]{0:T(512)(128)(4,1)S(1)} %dynamic-slice_reduce_fusion.5, bf16[512,3,12,64]{0,3,2,1:T(8,128)(2,1)S(1)} %dynamic-slice_bitcast_fusion.7, ...), kind=kOutput, calls=%fused_computation.17.clone.1 | convolution fusion | flops 418375680 | bytes 26796548 | tf_op jit(solution)/shard_map/while/body/eval_jaxpr/qhd,khd->hqk/dot_general | solution.py:370
  347.3 7.1 %multiply_convert_fusion.5 = bf16[12,512,512]{1,2,0:T(8,128)(2,1)S(1)} fusion(f32[12,512,512]{1,2,0:T(8,128)} %get-tuple-element.310, f32[12,512,512]{1,2,0:T(8,128)S(1)} %fusion.102, f32[12,512]{1,0:T(8,128)S(1)} %get-tuple-element.311, f32[12,512]{1,0:T(8,128)S(1)} %dynamic-slice_bitcast_fusion.8, pred[512]{0:T(512)(128)(4,1)S(1)} %dynamic-slice_reduce_fusion.5), kind=kLoop, calls=%fused_computation.16.clone.1 | loop fusion | flops 18874368 | bytes 31506944 | tf_op jit(solution)/shard_map/while/body/eval_jaxpr/convert_element_type | solution.py:375
  366.2 7.3 %multiply_reduce_fusion.8 = (f32[12,512]{1,0:T(8,128)S(1)}, f32[12,512,512]{1,2,0:T(8,128)}) fusion(f32[12,512,512]{1,2,0:T(8,128)S(1)} %fusion.102, f32[12,512]{1,0:T(8,128)S(1)} %dynamic-slice_bitcast_fusion.8, pred[512]{0:T(512)(128)(4,1)S(1)} %dynamic-slice_reduce_fusion.5, bf16[512,3,12,64]{0,3,2,1:T(8,128)(2,1)S(1)} %dynamic-slice_bitcast_fusion.7, ...), kind=kOutput, calls=%fused_computation.17.clone.1 | convolution fusion | flops 418375680 | bytes 26796548 | tf_op jit(solution)/shard_map/while/body/eval_jaxpr/qhd,khd->hqk/dot_general | solution.py:370
  373.5 7.1 %multiply_convert_fusion.5 = bf16[12,512,512]{1,2,0:T(8,128)(2,1)S(1)} fusion(f32[12,512,512]{1,2,0:T(8,128)} %get-tuple-element.310, f32[12,512,512]{1,2,0:T(8,128)S(1)} %fusion.102, f32[12,512]{1,0:T(8,128)S(1)} %get-tuple-element.311, f32[12,512]{1,0:T(8,128)S(1)} %dynamic-slice_bitcast_fusion.8, pred[512]{0:T(512)(128)(4,1)S(1)} %dynamic-slice_reduce_fusion.5), kind=kLoop, calls=%fused_computation.16.clone.1 | loop fusion | flops 18874368 | bytes 31506944 | tf_op jit(solution)/shard_map/while/body/eval_jaxpr/convert_element_type | solution.py:375
  388.7 7.0 %copy.133 = bf16[2,512,2304]{2,1,0:T(8,128)(2,1)} copy(bf16[2,512,2304]{1,2,0:T(8,128)(2,1)} %get-tuple-element.69) | data formatting | bytes 9437184 | tf_op jit(solution)/shard_map/while | solution.py:459
  395.8 8.5 %add_convert_fusion.2 = bf16[1024,768]{0,1:T(8,128)(2,1)} fusion(f32[1024,768]{0,1:T(8,128)S(1)} %copy-done.5, bf16[1024,2304]{1,0:T(8,128)(2,1)} %bitcast.267, f32[1024]{0:T(1024)S(1)} %copy-done.50, bf16[768,768]{1,0:T(8,128)(2,1)} %bitcast.293, bf16[768,768]{1,0:T(8,128)(2,1)} %bitcast.295, bf16[768,768]{1,0:T(8,128)(2,1)} %bitcast.297), kind=kOutput, calls=%fused_computation.79 | convolution fusion | flops 3636854784 | bytes 12980224 | tf_op jit(solution)/shard_map/dot_general | solution.py:336
  404.4 5.4 fusion.35
  411.6 38.8 %all-reduce.1 = f32[9216]{0:T(1024)S(1)} all-reduce(f32[9216]{0:T(1024)S(1)} %constant_dynamic-update-slice_fusion.19), channel_id=2, replica_groups=mesh['dp'=8,'inner'=4] {'dp','inner'}, use_global_device_ids=true, to_apply=%region_23.24.clone | all-reduce | flops 9216 | bytes 73728
  456.6 3.6 convert_element_type.331
  469.5 3.7 convert_element_type.325
  479.7 5.1 copy-done.3
  484.8 69.2 %shard_map.154 = f32[12,24,768]{2,1,0:T(8,128)S(1)} custom-call(bf16[12,2,2,2,2,2,16,1152]{7,6,5,4,3,2,1,0:T(8,128)(2,1)} %copy-done.3), custom_call_target="tpu_custom_call" | custom-call | tf_op jit(solution)/shard_map/pallas_call | solution.py:256
  (260 shorter events, 130.3 us)
Async XLA Ops:
  0.6 51.7 %copy-start = (bf16[2,128,768]{2,1,0:T(8,128)(2,1)S(1)}, bf16[2,128,768]{2,1,0:T(8,128)(2,1)}, u32[]{:S(2)}) copy-start(bf16[2,128,768]{2,1,0:T(8,128)(2,1)} %param.23) | copy-start | bytes 1179652
  0.6 50.1 %copy-start.21 = (bf16[1024,768]{1,0:T(8,128)(2,1)S(1)}, bf16[1024,768]{1,0:T(8,128)(2,1)}, u32[]{:S(2)}) copy-start(bf16[1024,768]{1,0:T(8,128)(2,1)} %param.14) | copy-start | bytes 4718596
  0.7 51.7 %copy-start.60 = (s32[2,128]{1,0:T(2,128)S(1)}, s32[2,128]{1,0:T(2,128)}, u32[]{:S(2)}) copy-start(s32[2,128]{1,0:T(2,128)} %param.22) | copy-start | bytes 3076
  157.5 27.2 %copy-start.57 = (f32[768]{0:T(1024)S(1)}, f32[768]{0:T(1024)}, u32[]{:S(2)}) copy-start(f32[768]{0:T(1024)} %get-tuple-element.223) | copy-start | bytes 9220
  184.8 43.7 %slice-start = ((s8[4718592]{0:T(1024)(128)(4,1)}), s8[4194304]{0:T(1024)(128)(4,1)S(1)}, s32[]{:S(2)}) async-start(s8[4718592]{0:T(1024)(128)(4,1)} %bitcast.263), calls=%async_computation | async-start | bytes 8388608
  188.7 85.9 %copy-start.6 = (f32[1024,768]{0,1:T(8,128)}, f32[1024,768]{0,1:T(8,128)S(1)}, u32[]{:S(2)}) copy-start(f32[1024,768]{0,1:T(8,128)S(1)} %get-tuple-element.227) | copy-start | bytes 9437188
  189.1 39.3 %copy-start.41 = (f32[1024]{0:T(1024)}, f32[1024]{0:T(1024)S(1)}, u32[]{:S(2)}) copy-start(f32[1024]{0:T(1024)S(1)} %multiply_reduce_fusion.6) | copy-start | bytes 12292
  189.2 39.2 %slice-start.1 = ((s8[4718592]{0:T(1024)(128)(4,1)}), s8[524288]{0:T(1024)(128)(4,1)S(1)}, s32[]{:S(2)}) async-start(s8[4718592]{0:T(1024)(128)(4,1)} %bitcast.263), calls=%async_computation.1 | async-start | bytes 1048576
  189.2 39.2 %copy-start.56 = (f32[768]{0:T(1024)S(1)}, f32[768]{0:T(1024)}, u32[]{:S(2)}) copy-start(f32[768]{0:T(1024)} %get-tuple-element.220) | copy-start | bytes 9220
  228.4 8.1 %copy-start.44 = (f32[768]{0:T(1024)S(1)}, f32[768]{0:T(1024)}, u32[]{:S(2)}) copy-start(f32[768]{0:T(1024)} %get-tuple-element.218) | copy-start | bytes 9220
  265.6 9.0 %copy-start.8 = (f32[1024,768]{0,1:T(8,128)S(1)}, f32[1024,768]{0,1:T(8,128)}, u32[]{:S(2)}) copy-start(f32[1024,768]{0,1:T(8,128)} %get-tuple-element.176) | copy-start | bytes 9437188
  265.6 9.0 %copy-start.30 = (bf16[1,2,2,2,2,48,768]{6,5,4,3,2,1,0:T(8,128)(2,1)S(1)}, bf16[1,2,2,2,2,48,768]{6,5,4,3,2,1,0:T(8,128)(2,1)}, u32[]{:S(2)}) copy-start(bf16[1,2,2,2,2,48,768]{6,5,4,3,2,1,0:T(8,128)(2,1)} %get-tuple-element.183) | copy-start | bytes 3538948
  265.6 9.0 %copy-start.32 = (bf16[1,2,2,2,2,48,768]{6,5,4,3,2,1,0:T(8,128)(2,1)S(1)}, bf16[1,2,2,2,2,48,768]{6,5,4,3,2,1,0:T(8,128)(2,1)}, u32[]{:S(2)}) copy-start(bf16[1,2,2,2,2,48,768]{6,5,4,3,2,1,0:T(8,128)(2,1)} %get-tuple-element.184) | copy-start | bytes 3538948
  265.6 9.0 %copy-start.34 = (bf16[1,2,2,2,2,48,768]{6,5,4,3,2,1,0:T(8,128)(2,1)S(1)}, bf16[1,2,2,2,2,48,768]{6,5,4,3,2,1,0:T(8,128)(2,1)}, u32[]{:S(2)}) copy-start(bf16[1,2,2,2,2,48,768]{6,5,4,3,2,1,0:T(8,128)(2,1)} %get-tuple-element.185) | copy-start | bytes 3538948
  265.7 9.0 %copy-start.36 = (bf16[1,2,2,2,2,48,768]{6,5,4,3,2,1,0:T(8,128)(2,1)S(1)}, bf16[1,2,2,2,2,48,768]{6,5,4,3,2,1,0:T(8,128)(2,1)}, u32[]{:S(2)}) copy-start(bf16[1,2,2,2,2,48,768]{6,5,4,3,2,1,0:T(8,128)(2,1)} %get-tuple-element.186) | copy-start | bytes 3538948
  274.7 10.9 %copy-start.42 = (f32[1024]{0:T(1024)S(1)}, f32[1024]{0:T(1024)}, u32[]{:S(2)}) copy-start(f32[1024]{0:T(1024)} %copy-done.41) | copy-start | bytes 12292
  292.7 32.7 %copy-start.4 = (f32[1024,768]{0,1:T(8,128)}, f32[1024,768]{0,1:T(8,128)S(1)}, u32[]{:S(2)}) copy-start(f32[1024,768]{0,1:T(8,128)S(1)} %get-tuple-element.174) | copy-start | bytes 9437188
  302.3 23.2 %copy-start.49 = (f32[1024]{0:T(1024)}, f32[1024]{0:T(1024)S(1)}, u32[]{:S(2)}) copy-start(f32[1024]{0:T(1024)S(1)} %negate_multiply_fusion.1) | copy-start | bytes 12292
  388.7 7.1 %copy-start.5 = (f32[1024,768]{0,1:T(8,128)S(1)}, f32[1024,768]{0,1:T(8,128)}, u32[]{:S(2)}) copy-start(f32[1024,768]{0,1:T(8,128)} %copy-done.4) | copy-start | bytes 9437188
  388.7 7.1 %copy-start.50 = (f32[1024]{0:T(1024)S(1)}, f32[1024]{0:T(1024)}, u32[]{:S(2)}) copy-start(f32[1024]{0:T(1024)} %copy-done.49) | copy-start | bytes 12292
  395.7 8.5 %copy-start.9 = (bf16[2,512,2304]{2,1,0:T(8,128)(2,1)S(1)}, bf16[2,512,2304]{2,1,0:T(8,128)(2,1)}, u32[]{:S(2)}) copy-start(bf16[2,512,2304]{2,1,0:T(8,128)(2,1)} %copy.133) | copy-start | bytes 14155780
  395.7 8.5 %copy-start.22 = (bf16[1024,768]{1,0:T(8,128)(2,1)S(1)}, bf16[1024,768]{1,0:T(8,128)(2,1)}, u32[]{:S(2)}) copy-start(bf16[1024,768]{1,0:T(8,128)(2,1)} %param.14) | copy-start | bytes 4718596
  404.3 7.1 %copy-start.43 = (f32[9216]{0:T(1024)S(1)}, f32[9216]{0:T(1024)}, u32[]{:S(2)}) copy-start(f32[9216]{0:T(1024)} %custom-call) | copy-start | bytes 110596
  404.3 7.1 %copy-start.51 = (f32[768]{0:T(1024)S(1)}, f32[768]{0:T(1024)}, u32[]{:S(2)}) copy-start(f32[768]{0:T(1024)} %get-tuple-element.171) | copy-start | bytes 9220
  404.3 7.1 %copy-start.59 = (f32[768]{0:T(1024)S(1)}, f32[768]{0:T(1024)}, u32[]{:S(2)}) copy-start(f32[768]{0:T(1024)} %get-tuple-element.144) | copy-start | bytes 9220
  404.3 7.1 %copy-start.58 = (f32[768]{0:T(1024)S(1)}, f32[768]{0:T(1024)}, u32[]{:S(2)}) copy-start(f32[768]{0:T(1024)} %get-tuple-element.146) | copy-start | bytes 9220
  404.3 7.1 %copy-start.54 = (f32[3072]{0:T(1024)S(1)}, f32[3072]{0:T(1024)}, u32[]{:S(2)}) copy-start(f32[3072]{0:T(1024)} %get-tuple-element.232) | copy-start | bytes 36868
  404.3 7.2 %copy-start.48 = (f32[768]{0:T(1024)S(1)}, f32[768]{0:T(1024)}, u32[]{:S(2)}) copy-start(f32[768]{0:T(1024)} %get-tuple-element.169) | copy-start | bytes 9220
  404.3 7.2 %copy-start.52 = (f32[768]{0:T(1024)S(1)}, f32[768]{0:T(1024)}, u32[]{:S(2)}) copy-start(f32[768]{0:T(1024)} %get-tuple-element.142) | copy-start | bytes 9220
  404.4 7.2 %copy-start.47 = (f32[768]{0:T(1024)S(1)}, f32[768]{0:T(1024)}, u32[]{:S(2)}) copy-start(f32[768]{0:T(1024)} %get-tuple-element.234) | copy-start | bytes 9220
  468.0 6.7 %copy-start.17 = (bf16[16,2,3,8,2,384]{5,3,2,4,0,1:T(8,128)(2,1)S(1)}, bf16[16,2,3,8,2,384]{5,3,2,4,0,1:T(8,128)(2,1)}, u32[]{:S(2)}) copy-start(bf16[16,2,3,8,2,384]{5,3,2,4,0,1:T(8,128)(2,1)} %copy.135) | copy-start | bytes 3538948
  484.8 72.2 %copy-start.1 = (bf16[2,128,768]{2,1,0:T(8,128)(2,1)S(1)}, bf16[2,128,768]{2,1,0:T(8,128)(2,1)}, u32[]{:S(2)}) copy-start(bf16[2,128,768]{2,1,0:T(8,128)(2,1)} %param.23) | copy-start | bytes 1179652
  (31 other events, 92.8 us)

commit v2 on v0

v2 whole, which is shorter than its diff:
```python
from functools import partial

import jax
import jax.numpy as jnp
from jax import lax
from jax.experimental import pallas as pl
from jax.experimental.pallas import tpu as pltpu
from jax.sharding import PartitionSpec as P

D = 768
H = 12
HD = 64
FF = 3072
SEQ_LEN = 512
PMAX = 128
norm_eps = 1e-05
masked_score = -1e30

bf = jnp.bfloat16
f32 = jnp.float32
MESH = pl.DeviceIdType.MESH
PARTS = 32
ROWS = D // PARTS
UNITS = 12
K_UNIT, V_UNIT, Q_UNIT, OUT_UNIT, UP_UNIT, DOWN_UNIT = 0, 1, 2, 3, 4, 8
CORE, X, Y, Z0, Z1 = range(5)
ALL = slice(None)
HALF = D // 2
WIRE = 3 * HALF

gather_types = (
    "ab", "ab", "ab", "ab", "ab", "e", "f", "e", "f", "e", "f", "ab",
)
gather_order = (
    "0z1", "1z1", "2z1", "11z1", "8s0", "6s0", "10s0", "5s0", "9s0", "7s0", "0z0", "1z0", "3z1",
    "0B1", "0A1", "2z0", "8z1", "4z1", "1B1", "1A1", "0B2", "0A2", "2B1", "11z0", "1A2", "3z0",
    "2A1", "1B2", "4z0", "7z1", "6z1", "0C", "2A2", "4B1", "2B2", "3B1", "7z0", "11B1", "3A1",
    "1C", "11A1", "8z0", "2C", "4A1", "3A2", "6z0", "5z1", "9z1", "3B2", "7s3", "4A2", "10z1",
    "4B2", "8s3", "5z0", "3C", "9z0", "6s3", "7C", "5s3", "4C", "10z0", "9s3", "8C", "11B2",
    "10s3", "11A2", "5C", "6C", "9C", "10C", "11C",
)
gather_counts = (
    10, 0, 0, 0, 0, 23, 0, 3, 6, 0, 2, 6, 0, 0, 4, 0, 0, 2, 2, 0, 1, 1, 2, 3, 0, 2, 2, 0, 0, 0, 0,
)
scatter_units = (4, 5, 6, 7, 8, 9, 10, 11, 3, 1, 0, 2)
scatter_types = (
    "f", "e", "f", "e", "f", "e", "ab", "ab", "ab", "ab", "ab", "ab",
)
scatter_order = (
    "0C", "1C", "0s3", "3C", "1s3", "4C", "2C", "4s3", "7C", "3s3", "5C", "7A2", "8C", "6C", "2s3",
    "0z0", "8B2", "7B2", "5s3", "1z0", "4z0", "8A2", "8B1", "3z0", "9C", "6A2", "0z1", "10C",
    "11C", "6B2", "11A2", "4z1", "2z0", "11B2", "1z1", "8A1", "3z1", "6B1", "6A1", "5z0", "11B1",
    "7A1", "11A1", "9A2", "9B2", "8z0", "2z1", "10B2", "6z0", "7B1", "8z1", "11z0", "5z1", "10A2",
    "7z0", "3s0", "9B1", "11z1", "9A1", "6z1", "10A1", "10B1", "7z1", "4s0", "2s0", "9z0", "5s0",
    "1s0", "10z0", "0s0", "9z1", "10z1",
)
scatter_counts = (
    0, 1, 1, 1, 4, 0, 0, 4, 0, 0, 5, 0, 0, 4, 2, 0, 0, 0, 0, 6, 2, 0, 0, 0, 0, 0, 7, 0, 0, 0, 3, 5,
    3, 2, 1, 5, 1, 3, 2, 6, 2, 1, 1,
)


def parse(order):
    digits = [2 if o[1].isdigit() else 1 for o in order]
    return [(int(o[:d]), o[d:]) for o, d in zip(order, digits)]


class Place:
    def __init__(self, dp_size, inner_size):
        self.sub_size = dp_size * inner_size // PARTS
        self.inner_size = inner_size
        number = lax.axis_index("dp") * inner_size + lax.axis_index("inner")
        self.sub = number % self.sub_size
        self.group = number // self.sub_size
        self.bits = [(self.group // 2**b) % 2 for b in range(5)]
        self.c, self.x, self.y, self.z0, self.z1 = self.bits

    def partner(self, b):
        group = self.group + 2**b - 2 * 2**b * self.bits[b]
        number = group * self.sub_size + self.sub
        return (number // self.inner_size, number % self.inner_size)


def remote(src, dst, send_sem, recv_sem, device):
    return pltpu.make_async_remote_copy(
        src_ref=src,
        dst_ref=dst,
        send_sem=send_sem,
        recv_sem=recv_sem,
        device_id=device,
        device_id_type=MESH,
    )


def enter(place):
    barrier = pltpu.get_barrier_semaphore()
    for b in range(5):
        pl.semaphore_signal(barrier, inc=1, device_id=place.partner(b), device_id_type=MESH)
    pl.semaphore_wait(barrier, 5)


class Gather:
    def __init__(self, place, W, send, recv):
        self.place, self.W, self.send, self.recv = place, W, send, recv
        self.cols = pl.ds(pl.multiple_of(HALF * place.c, 128), HALF)
        x, y, z0, z1 = place.x, place.y, place.z0, place.z1
        every = (ALL, ALL, ALL, ALL)
        self.legs = {
            "ab": [
                ("z1", (), Z1, (z1, z0, y, x)),
                ("z0", ("z1",), Z0, (ALL, z0, y, x)),
                ("A1", ("z0",), Y, (0, ALL, y, x)),
                ("B1", ("z0",), X, (1, ALL, y, x)),
                ("A2", ("A1",), X, (0, ALL, ALL, x)),
                ("B2", ("B1",), Y, (1, ALL, y, ALL)),
                ("C", ("A2", "B2"), CORE, every),
            ],
            "e": [
                ("s0", (), X, (z1, z0, y, x)),
                ("z1", ("s0",), Z1, (z1, z0, y, ALL)),
                ("z0", ("z1",), Z0, (ALL, z0, y, ALL)),
                ("s3", ("z0",), Y, (ALL, ALL, y, ALL)),
                ("C", ("s3",), CORE, every),
            ],
            "f": [
                ("s0", (), Y, (z1, z0, y, x)),
                ("z1", ("s0",), Z1, (z1, z0, ALL, x)),
                ("z0", ("z1",), Z0, (ALL, z0, ALL, x)),
                ("s3", ("z0",), X, (ALL, ALL, ALL, x)),
                ("C", ("s3",), CORE, every),
            ],
        }
        self.got, self.sent = set(), []

    def copy(self, m, name):
        legs = self.legs[gather_types[m]]
        k = [leg[0] for leg in legs].index(name)
        _, after, b, index = legs[k]
        part = self.W.at[(m,) + index + (ALL, self.cols)]
        sems = self.send.at[m, k], self.recv.at[m, k]
        return remote(part, part, *sems, self.place.partner(b)), after

    def arrive(self, m, name="C"):
        if (m, name) not in self.got:
            self.got.add((m, name))
            self.copy(m, name)[0].wait_recv()

    def op(self, m, name):
        copy, after = self.copy(m, name)
        for a in after:
            self.arrive(m, a)
        copy.start()
        self.sent.append((m, name))

    def drain(self):
        for m, name in self.sent:
            self.copy(m, name)[0].wait_send()


class Scatter:
    def __init__(self, place, S, R, send, recv, ready, order):
        self.place, self.S, self.R = place, S, R
        self.send, self.recv, self.ready = send, recv, ready
        x, y, z0, z1 = place.x, place.y, place.z0, place.z1
        self.legs = {
            "ab": [
                ("A2", ("C",), X, (0, ALL, ALL, 1 - x), (0, ALL, ALL, 1 - x), (0, ALL, ALL, x), (0, ALL, ALL, x)),
                ("B2", ("C",), Y, (1, ALL, 1 - y, ALL), (1, ALL, 1 - y, ALL), (1, ALL, y, ALL), (1, ALL, y, ALL)),
                ("A1", ("A2",), Y, (0, ALL, 1 - y, x), (0, ALL, 1 - y, 1 - x), (0, ALL, y, x), (0, ALL, y, 1 - x)),
                ("B1", ("B2",), X, (1, ALL, y, 1 - x), (1, ALL, 1 - y, 1 - x), (1, ALL, y, x), (1, ALL, 1 - y, x)),
                ("z0", ("A1", "B1"), Z0, (ALL, 1 - z0, y, x), (ALL, 1 - z0, 1 - y, 1 - x), (ALL, z0, y, x), (ALL, z0, 1 - y, 1 - x)),
                ("z1", ("z0",), Z1, (1 - z1, z0, y, x), (1 - z1, 1 - z0, 1 - y, 1 - x), (z1, z0, y, x), (z1, 1 - z0, 1 - y, 1 - x)),
            ],
            "e": [
                ("s3", ("C",), Y, (ALL, ALL, 1 - y, ALL), (ALL, ALL, 1 - y, ALL), (ALL, ALL, y, ALL), (ALL, ALL, y, ALL)),
                ("z0", ("s3",), Z0, (ALL, 1 - z0, y, ALL), (ALL, 1 - z0, 1 - y, ALL), (ALL, z0, y, ALL), (ALL, z0, 1 - y, ALL)),
                ("z1", ("z0",), Z1, (1 - z1, z0, y, ALL), (1 - z1, 1 - z0, 1 - y, ALL), (z1, z0, y, ALL), (z1, 1 - z0, 1 - y, ALL)),
                ("s0", ("z1",), X, (z1, z0, y, 1 - x), (1 - z1, 1 - z0, 1 - y, 1 - x), (z1, z0, y, x), (1 - z1, 1 - z0, 1 - y, x)),
            ],
            "f": [
                ("s3", ("C",), X, (ALL, ALL, ALL, 1 - x), (ALL, ALL, ALL, 1 - x), (ALL, ALL, ALL, x), (ALL, ALL, ALL, x)),
                ("z0", ("s3",), Z0, (ALL, 1 - z0, ALL, x), (ALL, 1 - z0, ALL, 1 - x), (ALL, z0, ALL, x), (ALL, z0, ALL, 1 - x)),
                ("z1", ("z0",), Z1, (1 - z1, z0, ALL, x), (1 - z1, 1 - z0, ALL, 1 - x), (z1, z0, ALL, x), (z1, 1 - z0, ALL, 1 - x)),
                ("s0", ("z1",), Y, (z1, z0, 1 - y, x), (1 - z1, 1 - z0, 1 - y, 1 - x), (z1, z0, y, x), (1 - z1, 1 - z0, y, 1 - x)),
            ],
        }
        self.got, self.sent = set(), []
        self.turn = {}
        for m, name in order:
            if "C" in self.leg(m, name)[1] and m not in self.turn:
                self.turn[m] = len(self.turn)
        self.heard = {b: 0 for b in (X, Y, Z0, Z1)}

    def leg(self, m, name):
        if name == "C":
            return ("C", (), CORE)
        return [leg for leg in self.legs[scatter_types[m]] if leg[0] == name][0]

    def copy(self, m, name):
        c = self.place.c
        if name == "C":
            sems = self.send.at[m, 0], self.recv.at[m, 0]
            return remote(self.S.at[m, 1 - c], self.R.at[m], *sems, self.place.partner(CORE))
        k = [leg[0] for leg in self.legs[scatter_types[m]]].index(name) + 1
        _, _, b, out, land, _, _ = self.leg(m, name)
        sems = self.send.at[m, k], self.recv.at[m, k]
        return remote(
            self.S.at[(m, c) + out], self.S.at[(m, 1 - c) + land], *sems, self.place.partner(b)
        )

    def add(self, m, name):
        if (m, name) in self.got:
            return
        self.got.add((m, name))
        c = self.place.c
        copy = self.copy(m, name)
        if name == "C":
            copy.wait_send()
            self.sent.remove((m, name))
            for b in (X, Y, Z0, Z1):
                pl.semaphore_signal(
                    self.ready.at[b - 1],
                    inc=1,
                    device_id=self.place.partner(b),
                    device_id_type=MESH,
                )
            copy.wait_recv()
            self.S[m, c] = self.S[m, c] + self.R[m]
            return
        copy.wait_recv()
        own, landed = self.leg(m, name)[5:]
        self.S[(m, c) + own] = self.S[(m, c) + own] + self.S[(m, 1 - c) + landed]

    def op(self, m, name):
        after, b = self.leg(m, name)[1:3]
        for a in after:
            self.add(m, a)
        if b != CORE:
            need = self.turn[m] + 1 - self.heard[b]
            if need > 0:
                pl.semaphore_wait(self.ready.at[b - 1], need)
                self.heard[b] += need
        self.copy(m, name).start()
        self.sent.append((m, name))

    def last(self, m):
        name = self.legs[scatter_types[m]][-1][0]
        self.copy(m, name).wait_recv()
        c = self.place.c
        own, landed = self.leg(m, name)[5:]
        total = self.S[(m, c) + own].astype(f32) + self.S[(m, 1 - c) + landed].astype(f32)
        left, right = total[:8], total[8:]
        rows = [
            jnp.concatenate([v[:, HALF * k : HALF * k + HALF] for v in (left, right)], 1)
            for k in range(3)
        ]
        return jnp.concatenate(rows, 0)

    def drain(self):
        for m, name in self.sent:
            self.copy(m, name).wait_send()
        for b in (X, Y, Z0, Z1):
            if UNITS > self.heard[b]:
                pl.semaphore_wait(self.ready.at[b - 1], UNITS - self.heard[b])


def wire(rows):
    halves = [
        jnp.concatenate([rows[8 * k : 8 * k + 8, h * HALF : h * HALF + HALF] for k in range(3)], 1)
        for h in range(2)
    ]
    return jnp.concatenate(halves, 0).astype(bf)


def dot(left, right, left_axis, right_axis):
    return lax.dot_general(
        left,
        right,
        (((left_axis,), (right_axis,)), ((), ())),
        preferred_element_type=f32,
    )


def norm(rows):
    centered = rows - jnp.mean(rows, -1, keepdims=True)
    rstd = lax.rsqrt(jnp.mean(centered * centered, -1, keepdims=True) + norm_eps)
    return centered * rstd, rstd


def norm_back(grad, rhat, rstd):
    inner = jnp.mean(grad * rhat, -1, keepdims=True)
    return rstd * (grad - jnp.mean(grad, -1, keepdims=True) - rhat * inner)


def col_sum(rows):
    return jnp.sum(rows.astype(f32), 0, keepdims=True)


def gelu_parts(u):
    phi = 0.5 + 0.5 * lax.erf(u * 0.7071067811865476)
    return u * phi, phi, jnp.exp(-0.5 * u * u) * 0.3989422804014327


class Schedule:
    def __init__(self, engine, order, counts):
        self.engine, self.order, self.counts = engine, list(order), list(counts)

    def run(self, n):
        for _ in range(n):
            m, name = self.order.pop(0)
            self.engine.op(m, name)

    def before(self):
        self.run(self.counts.pop(0))

    def loop(self, n, body, needs=None):
        counts = [self.counts.pop(0) for _ in range(n)]

        @pl.loop(0, n)
        def _(i):
            for k in range(n):
                if counts[k] or needs:

                    @pl.when(i == k)
                    def _():
                        self.run(counts[k])
                        if needs:
                            needs(k)

            body(i)

    def rest(self):
        self.run(len(self.order))


def layer_kernel(
    sizes,
    lengths, counts, positions, vec_in, wq, wo, w1, w2, x_in, gv_in,
    layer_out, input_grad, g_qkv, g_out, g_up, g_down, g_vec,
    W, S, R, xs, J, ctx_t, act_g, slope_g, pick_t, pick, x_g, q_g, r1_g, n1_g, nl_g, d_two, d_one,
    f_grad, a_grad, c_grad, dq_g, ctx_gt, acc, n1_t, nl_t, out_t, gv, own_f, oth_f, vec_all, vec, vgrad,
    vsum, vland,
    g_send, g_recv, s_send, s_recv, ready, first, in_sem, out_sem, v_send, v_recv,
):
    place = Place(*sizes)
    c = place.c
    chip = (place.z1, place.z0, place.y, place.x)
    load_x = pltpu.make_async_copy(x_in, xs, in_sem.at[0])
    load_x.start()
    load_gv = pltpu.make_async_copy(gv_in, gv, in_sem.at[1])
    load_gv.start()
    G = Gather(place, W, g_send, g_recv)
    for u, src, at in (
        [(K_UNIT, wq, D), (V_UNIT, wq, 2 * D), (Q_UNIT, wq, 0), (OUT_UNIT, wo, 0)]
        + [(UP_UNIT + j, w1, D * j) for j in range(4)]
    ):
        own_f[u] = src[:, at : at + D].astype(f32)
    enter(place)
    other = pl.ds(pl.multiple_of(HALF * (1 - c), 128), HALF)
    pair = place.partner(CORE)
    halves = remote(own_f.at[:, :, other], oth_f, first.at[0], first.at[1], pair)
    halves.start()

    def vec_hop(b):
        at = [place.z1, place.z0, place.y, place.x, c]
        for done in vec_order[: vec_order.index(b)]:
            at[4 - done] = ALL
        part = vec_all.at[tuple(at)]
        return remote(part, part, v_send.at[b], v_recv.at[b], place.partner(b))

    vec_order = (CORE, X, Y, Z0, Z1)
    vec_all[tuple(chip) + (c,)] = vec_in[...]
    vec_hop(CORE).start()
    downs = []
    for j in range(2):
        at = (DOWN_UNIT + 2 * c + j,) + chip
        down = remote(w2.at[48 * j : 48 * j + 48, other], W.at[at + (ALL, other)], first.at[2 + 2 * j], first.at[3 + 2 * j], pair)
        down.start()
        downs.append(down)
        W[at + (ALL, G.cols)] = w2[48 * j : 48 * j + 48, G.cols]
    halves.wait_recv()
    for u in range(8):
        own, oth = own_f[u, :, G.cols], oth_f[u]
        low = jnp.where(c == 0, own, oth)
        high = jnp.where(c == 0, oth, own)
        W[(u,) + chip + (ALL, G.cols)] = jnp.concatenate([low, high], 0).astype(bf)
    for down in downs:
        down.wait_recv()
    plan = Schedule(G, parse(gather_order), gather_counts)
    for k in range(5):
        plan.before()
        vec_hop(vec_order[k]).wait_recv()
        if k < 4:
            vec_hop(vec_order[k + 1]).start()
    gathered = jnp.sum(vec_all[...].astype(f32).reshape(8, 4, 16, 128), 1)
    for r in range(72):
        vec[r // 6 : r // 6 + 1, 128 * (r % 6) : 128 * (r % 6) + 128] = gathered[r // 9, r % 9 : r % 9 + 1]

    def bias(i):
        return vec[pl.ds(i, 1), :]

    def unit(u):
        return W[u].reshape(D, D)

    def down_block(j):
        parts = [W[DOWN_UNIT + q, j // 2, j % 2, y, x] for y in range(2) for x in range(2) for q in range(4)]
        return jnp.concatenate(parts, 0)

    load_x.wait()
    load_gv.wait()
    for s in range(2):
        place_id = lax.broadcasted_iota(jnp.int32, (SEQ_LEN, PMAX), 0)
        slot_id = lax.broadcasted_iota(jnp.int32, (SEQ_LEN, PMAX), 1)
        match = (positions[s : s + 1, :] == place_id) & (slot_id < counts[s])
        hot = jnp.where(match, 1.0, 0.0)
        pick_t[s] = hot.astype(bf)
        pick[s] = hot.T.astype(bf)
        x_g[PMAX * s : PMAX * s + PMAX] = dot(pick[s], xs[SEQ_LEN * s : SEQ_LEN * s + SEQ_LEN], 1, 0).astype(bf)

    def project(i, u, b):
        def body(t):
            rows = pl.ds(pl.multiple_of(512 * t, 512), 512)
            y = dot(xs[rows, :], unit(u), 1, 0)
            J[i, rows, :] = (y if b is None else y + bias(b)).astype(bf)

        plan.before()
        G.arrive(u)
        plan.loop(2, body)

    project(1, K_UNIT, None)
    project(2, V_UNIT, 1)
    project(0, Q_UNIT, 0)

    lane_id = lax.broadcasted_iota(jnp.int32, (SEQ_LEN, 128), 1)
    key_id = lax.broadcasted_iota(jnp.int32, (SEQ_LEN, 128), 0)
    scale = bf(HD**-0.5)

    def pair_at(it):
        s, p = it // 6, it % 6
        rows = pl.ds(pl.multiple_of(s * SEQ_LEN, SEQ_LEN), SEQ_LEN)
        cols = pl.ds(pl.multiple_of(p * 128, 128), 128)
        mask = jnp.where(key_id < lengths[s], 0.0, masked_score).astype(bf)
        return s, rows, cols, mask

    def attend(it):
        s, rows, cols, mask = pair_at(it)
        q, k, v = J[0, rows, cols], J[1, rows, cols] * scale, J[2, rows, cols]
        v_t = v.T
        for h in range(2):
            mine = lane_id // HD == h
            scores = dot(jnp.where(mine, k, mask), jnp.where(mine, q, bf(1 / HD)), 1, 1)
            e = jnp.exp(scores - jnp.max(scores, 0, keepdims=True))
            total = jnp.sum(e, 0, keepdims=True)
            o = dot(v_t[HD * h : HD * h + HD], e.astype(bf), 1, 0) * (1.0 / total)
            at = pl.multiple_of((it % 6) * 128 + HD * h, HD)
            ctx_t[pl.ds(at, HD), rows] = o.astype(bf)

    plan.loop(12, attend)

    plan.before()
    G.arrive(OUT_UNIT)
    for s in range(2):
        rows = slice(SEQ_LEN * s, SEQ_LEN * s + SEQ_LEN)
        slots = slice(PMAX * s, PMAX * s + PMAX)
        ctx_gt[:, slots] = dot(ctx_t[:, rows], pick[s], 1, 1).astype(bf)
        q_g[slots, :] = dot(pick[s], J[0, rows, :], 1, 0).astype(bf)
    r1 = x_g[...].astype(f32) + (dot(ctx_gt[...], unit(OUT_UNIT), 0, 0) + bias(2))
    r1_g[...] = r1
    n1 = norm(r1)[0] * bias(3) + bias(4)
    n1_g[...] = n1
    nl_g[...] = n1.astype(bf)

    def up_listed(q):
        cols = pl.ds(pl.multiple_of(D * q, D), D)
        u = dot(nl_g[...], unit(UP_UNIT + q), 1, 0) + bias(5 + q)
        a, phi, density = gelu_parts(u)
        act_g[:, cols] = a.astype(bf)
        slope_g[:, cols] = (phi + u * density).astype(bf)

    plan.loop(4, up_listed, lambda q: G.arrive(UP_UNIT + q))
    plan.rest()
    for u in range(DOWN_UNIT, UNITS):
        G.arrive(u)

    acc[...] = n1_g[...] + bias(9)

    @pl.loop(0, 4)
    def _(q):
        cols = pl.ds(pl.multiple_of(D * q, D), D)
        acc[...] += dot(act_g[:, cols], down_block(q), 1, 0)

    rhat, rstd = norm(acc[...])
    used = [jnp.sum(pick[s].astype(f32), 1, keepdims=True) for s in range(2)]
    cot = jnp.where(jnp.concatenate(used, 0) > 0.5, gv[...].astype(f32), 0.0)
    vgrad[10:11, :] = col_sum(cot * rhat)
    vgrad[11:12, :] = col_sum(cot)
    two = norm_back(cot * bias(10), rhat, rstd)
    d_two[...] = two
    f_grad[...] = two.astype(bf)
    vgrad[9:10, :] = col_sum(f_grad[...])

    T = Scatter(place, S, R, s_send, s_recv, ready, parse(scatter_order))
    plan = Schedule(T, parse(scatter_order), scatter_counts)
    message = {u: m for m, u in enumerate(scatter_units)}

    def put(m, grad):
        for i in range(PARTS):
            S[m, i % 2, i // 16, i // 8 % 2, i // 4 % 2, i // 2 % 2] = wire(grad[ROWS * i : ROWS * i + ROWS])

    def ffn_back(q):
        cols = pl.ds(pl.multiple_of(D * q, D), D)
        fg = f_grad[...]
        pre = (dot(fg, down_block(q), 1, 1) * slope_g[:, cols].astype(f32)).astype(bf)
        vgrad[pl.ds(5 + q, 1), :] = col_sum(pre)
        put(message[UP_UNIT] + q, dot(nl_g[...], pre, 0, 0))
        d_two[...] += dot(pre, unit(UP_UNIT + q), 1, 1)
        down = dot(act_g[:, cols], fg, 0, 0)
        for i in range(8):
            for t in range(4):
                at = 96 * i + ROWS * t
                S[message[DOWN_UNIT] + t, i % 2, q // 2, q % 2, i // 4, i // 2 % 2] = wire(down[at : at + ROWS])

    plan.loop(4, ffn_back)
    plan.before()
    rhat, rstd = norm(r1_g[...])
    g = d_two[...]
    vgrad[3:4, :] = col_sum(g * rhat)
    vgrad[4:5, :] = col_sum(g)
    one = norm_back(g * bias(3), rhat, rstd)
    d_one[...] = one
    a_grad[...] = one.astype(bf)
    vgrad[2:3, :] = col_sum(a_grad[...])
    put(message[OUT_UNIT], dot(ctx_gt[...], a_grad[...], 1, 0))
    c_grad[...] = dot(a_grad[...], unit(OUT_UNIT), 1, 1).astype(bf)

    slot_lane = lax.broadcasted_iota(jnp.int32, (PMAX, 128), 1)

    def attend_back(it):
        s, rows, cols, mask = pair_at(it)
        slots = pl.ds(pl.multiple_of(s * PMAX, PMAX), PMAX)
        q, g = q_g[slots, cols], c_grad[slots, cols]
        k, v = J[1, rows, cols] * scale, J[2, rows, cols]
        none = jnp.zeros_like(q)
        both = lambda t: jnp.concatenate(
            [jnp.where(slot_lane < HD, t, none), jnp.where(slot_lane < HD, none, t)], 0
        )
        q2, g2 = both(q), both(g)
        ones = jnp.full((2 * PMAX, 128), 1 / 128, bf)
        scores = dot(jnp.concatenate([k, mask], 1), jnp.concatenate([q2, ones], 1), 1, 1)
        e = jnp.exp(scores - jnp.max(scores, 0, keepdims=True))
        probs = e * (1.0 / jnp.sum(e, 0, keepdims=True))
        d_probs = dot(v, g2, 1, 1)
        row_dot = jnp.sum(probs * d_probs, 0, keepdims=True)
        d_scores = (probs * (d_probs - row_dot)).astype(bf)
        dv = dot(probs.astype(bf), g2, 1, 0)
        dk = dot(d_scores, q2 * scale, 1, 0)
        dq2 = dot(d_scores, k, 0, 0)
        dq = jnp.where(slot_lane < HD, dq2[:PMAX], dq2[PMAX:])
        dq_g[slots, cols] = dq.astype(bf)
        J[1, rows, cols] = dk.astype(bf)
        J[2, rows, cols] = dv.astype(bf)

    plan.loop(12, attend_back)
    plan.before()
    put(message[V_UNIT], dot(xs[...], J[2], 0, 0))
    vgrad[1:2, :] = col_sum(J[2])
    plan.before()
    put(message[K_UNIT], dot(xs[...], J[1], 0, 0))
    plan.before()
    put(message[Q_UNIT], dot(x_g[...], dq_g[...], 0, 0))
    vgrad[0:1, :] = col_sum(dq_g[...])

    for r in range(72):
        vsum[r // 36, r // 18 % 2, r // 9 % 2, r % 9 : r % 9 + 1] = vgrad[r // 6 : r // 6 + 1, 128 * (r % 6) : 128 * (r % 6) + 128]
    y, z0, z1 = place.y, place.z0, place.z1
    hops = [
        (CORE, (ALL, ALL, ALL), (ALL, ALL, ALL)),
        (X, (ALL, ALL, ALL), (ALL, ALL, ALL)),
        (Y, (ALL, ALL, 1 - y), (ALL, ALL, y)),
        (Z0, (ALL, 1 - z0, y), (ALL, z0, y)),
        (Z1, (1 - z1, z0, y), (z1, z0, y)),
    ]

    def hop(k):
        b, out, _ = hops[k]
        return remote(vsum.at[out], vland.at[(k,) + out], v_send.at[5 + k], v_recv.at[5 + k], place.partner(b))

    def take(k):
        copy = hop(k)
        copy.wait_send()
        copy.wait_recv()
        own = hops[k][2]
        vsum[own] = vsum[own] + vland[(k,) + own]

    for k in range(5):
        plan.before()
        if k > 0:
            take(k - 1)
        hop(k).start()

    def ffn_all(it):
        t, q = it // 4, it % 4
        rows = pl.ds(pl.multiple_of(256 * t, 256), 256)

        @pl.when(q == 0)
        def _():
            r = xs[rows, :].astype(f32) + (dot(ctx_t[:, rows], unit(OUT_UNIT), 0, 0) + bias(2))
            n = norm(r)[0] * bias(3) + bias(4)
            n1_t[...] = n
            nl_t[...] = n.astype(bf)
            acc[...] = n + bias(9)

        a = gelu_parts(dot(nl_t[...], unit(UP_UNIT + q), 1, 0) + bias(5 + q))[0]
        acc[...] += dot(a.astype(bf), down_block(q), 1, 0)

        @pl.when(q == 3)
        def _():
            done = pltpu.make_async_copy(out_t, layer_out.at[rows, :], out_sem.at[0])

            @pl.when(t > 0)
            def _():
                done.wait()

            out_t[...] = (norm(acc[...])[0] * bias(10) + bias(11)).astype(bf)
            done.start()

    plan.loop(16, ffn_all)
    take(4)
    g_vec[...] = vsum[z1, z0, y]

    def grad_in(s):
        rows = pl.ds(pl.multiple_of(s * SEQ_LEN, SEQ_LEN), SEQ_LEN)
        slots = pl.ds(pl.multiple_of(s * PMAX, PMAX), PMAX)
        t = d_one[slots, :] + dot(dq_g[slots, :], unit(Q_UNIT), 1, 1)
        high = t.astype(bf)
        low = (t - high.astype(f32)).astype(bf)
        total = dot(pick_t[s], high, 1, 0) + dot(pick_t[s], low, 1, 0)
        total += dot(J[1, rows, :], unit(K_UNIT), 1, 1)
        total += dot(J[2, rows, :], unit(V_UNIT), 1, 1)
        J[0, rows, :] = total.astype(bf)

    plan.loop(2, grad_in)
    store = pltpu.make_async_copy(J.at[0], input_grad, out_sem.at[1])
    store.start()
    plan.rest()
    for m, u in enumerate(scatter_units):
        grad = T.last(m)
        if u in (K_UNIT, V_UNIT, Q_UNIT):
            at = D * ((u + 1) % 3)
            g_qkv[:, at : at + D] = grad
        elif u == OUT_UNIT:
            g_out[...] = grad
        elif u < DOWN_UNIT:
            at = D * (u - UP_UNIT)
            g_up[:, at : at + D] = grad
        else:
            at = ROWS * (u - DOWN_UNIT)
            g_down[at : at + ROWS, :] = grad
    pltpu.make_async_copy(out_t, layer_out.at[0:256, :], out_sem.at[0]).wait()
    store.wait()
    halves.wait_send()
    for down in downs:
        down.wait_send()
    for b in vec_order:
        vec_hop(b).wait_send()
    G.drain()
    T.drain()


def layer_call(sizes, *args):
    vmem = pl.BlockSpec(memory_space=pltpu.VMEM)
    smem = pl.BlockSpec(memory_space=pltpu.SMEM)
    hbm = pl.BlockSpec(memory_space=pl.ANY)
    tokens = 2 * SEQ_LEN
    slots = 2 * PMAX
    dma = pltpu.SemaphoreType.DMA
    return pl.pallas_call(
        partial(layer_kernel, sizes),
        out_shape=(
            jax.ShapeDtypeStruct((tokens, D), bf),
            jax.ShapeDtypeStruct((tokens, D), bf),
            jax.ShapeDtypeStruct((ROWS, 3 * D), f32),
            jax.ShapeDtypeStruct((ROWS, D), f32),
            jax.ShapeDtypeStruct((ROWS, FF), f32),
            jax.ShapeDtypeStruct((FF // PARTS, D), f32),
            jax.ShapeDtypeStruct((16, 128), f32),
        ),
        in_specs=[smem, smem] + [vmem] * 6 + [hbm] * 2,
        out_specs=(hbm,) * 2 + (vmem,) * 5,
        scratch_shapes=[
            pltpu.VMEM((UNITS, 2, 2, 2, 2, 2 * ROWS, D), bf),
            pltpu.VMEM((UNITS, 2, 2, 2, 2, 2, 16, WIRE), bf),
            pltpu.VMEM((UNITS, 2, 2, 2, 2, 16, WIRE), bf),
            pltpu.VMEM((tokens, D), bf),
            pltpu.VMEM((3, tokens, D), bf),
            pltpu.VMEM((D, tokens), bf),
            pltpu.VMEM((slots, FF), bf),
            pltpu.VMEM((slots, FF), bf),
            pltpu.VMEM((2, SEQ_LEN, PMAX), bf),
            pltpu.VMEM((2, PMAX, SEQ_LEN), bf),
            pltpu.VMEM((slots, D), bf),
            pltpu.VMEM((slots, D), bf),
            pltpu.VMEM((slots, D), f32),
            pltpu.VMEM((slots, D), f32),
            pltpu.VMEM((slots, D), bf),
            pltpu.VMEM((slots, D), f32),
            pltpu.VMEM((slots, D), f32),
            pltpu.VMEM((slots, D), bf),
            pltpu.VMEM((slots, D), bf),
            pltpu.VMEM((slots, D), bf),
            pltpu.VMEM((slots, D), bf),
            pltpu.VMEM((D, slots), bf),
            pltpu.VMEM((256, D), f32),
            pltpu.VMEM((256, D), f32),
            pltpu.VMEM((256, D), bf),
            pltpu.VMEM((256, D), bf),
            pltpu.VMEM((slots, D), bf),
            pltpu.VMEM((8, ROWS, D), f32),
            pltpu.VMEM((8, ROWS, HALF), f32),
            pltpu.VMEM((2, 2, 2, 2, 2, 16, 128), bf),
            pltpu.VMEM((16, D), f32),
            pltpu.VMEM((16, D), f32),
            pltpu.VMEM((2, 2, 2, 16, 128), f32),
            pltpu.VMEM((5, 2, 2, 2, 16, 128), f32),
            dma((UNITS, 7)),
            dma((UNITS, 7)),
            dma((UNITS, 7)),
            dma((UNITS, 7)),
            pltpu.SemaphoreType.REGULAR((4,)),
            dma((6,)),
            dma((2,)),
            dma((2,)),
            dma((10,)),
            dma((10,)),
        ],
        compiler_params=pltpu.CompilerParams(
            collective_id=0, has_side_effects=True, vmem_limit_bytes=63 * 2**20
        ),
    )(*args)


def sub_groups(sizes):
    sub = sizes[0] * sizes[1] // PARTS
    return [[sub * i + j for j in range(sub)] for i in range(PARTS)]


def whole_group(sizes, flat):
    if sizes[0] * sizes[1] == PARTS:
        return flat
    return lax.all_gather(flat, ("dp", "inner"), axis_index_groups=sub_groups(sizes), tiled=True)


def own_part(sizes, flat):
    if sizes[0] * sizes[1] == PARTS:
        return flat
    return lax.psum_scatter(
        flat, ("dp", "inner"), axis_index_groups=sub_groups(sizes), scatter_dimension=0, tiled=True
    )


def on_device(
    sizes,
    inputs,
    qkv_weight,
    out_weight,
    up_weight,
    down_weight,
    vectors,
    lengths,
    counts,
    positions,
    grad_values,
):
    wq, wo, w1, w2, vec = [
        whole_group(sizes, w) for w in (qkv_weight, out_weight, up_weight, down_weight, vectors)
    ]
    number = lax.axis_index("dp") * sizes[1] + lax.axis_index("inner")
    quarter = number // (sizes[0] * sizes[1] // PARTS) % 4
    size = vec.shape[0]
    frame = jnp.where(jnp.arange(4 * size) // size == quarter, jnp.tile(vec, 4), bf(0))
    frame = jnp.pad(frame, (0, 16 * 128 - 4 * size)).reshape(16, 128)
    layer_out, input_grad, g_qkv, g_out, g_up, g_down, g_vec = layer_call(
        sizes,
        lengths,
        counts,
        positions,
        frame,
        wq.reshape(ROWS, 3 * D),
        wo.reshape(ROWS, D),
        w1.reshape(ROWS, FF),
        w2.reshape(FF // PARTS, D),
        inputs,
        grad_values.reshape(-1, D),
    )
    g_vec = lax.dynamic_slice(g_vec.reshape(-1), (quarter * size,), (size,))
    flat = [own_part(sizes, g.reshape(-1)) for g in (g_qkv, g_out, g_up, g_down, g_vec)]
    return (layer_out, input_grad, *flat)


def solution(mesh):
    both = ("dp", "inner")
    rows, flat = P(both, None), P(both)
    return jax.shard_map(
        partial(on_device, (mesh.shape["dp"], mesh.shape["inner"])),
        mesh=mesh,
        in_specs=(rows, flat, flat, flat, flat, flat, flat, flat, rows, P(both, None, None)),
        out_specs=(rows, rows, flat, flat, flat, flat, flat),
        check_vma=False,
    )
```

time: 900 us -> 189 us (0.21)
  waiting for transfers between devices: 455 us -> 0 us
  matrix products: 170 us -> 0 us
  Pallas kernels: 0 us -> 169 us
  local copies, waits for them, and re-layouts: 134 us -> 19 us
  blocking collectives: 83.9 us -> 0 us
  other arithmetic: 33.4 us -> 0.01 us
  between operations: 14.8 us -> 0.68 us
    unnamed x6 -> x0, waiting for transfers between devices: 373 us -> none
    dot_general x27 -> x0, matrix products: 170 us -> none  [the longest x4 58.2 us: matmul(): return jnp.dot(left, right, preferred_element_type=jnp.float32)]
    pallas_call x0 -> x1, Pallas kernels: none -> 169 us  [layer_call(): pl.pallas_call(partial(layer_kernel, sizes), out_shape=(jax.ShapeDtypeStr...]
    unnamed x2 -> x0, blocking collectives: 83.9 us -> none
    all_gather x4 -> x0, waiting for transfers between devices: 82.6 us -> none  [the longest x1 58.6 us: on_device(): lax.all_gather(qkv_weight, ('dp', 'inner'), axis=0, tiled=True)]
    reshape x10 -> x8, local copies, waits for them, and re-layouts: 61.6 us -> 11.9 us  [the longest x3 4.85 us: on_device(): g.reshape(-1)]
    unnamed x95 -> x7, local copies, waits for them, and re-layouts: 31.3 us -> 4.85 us
    reduce_sum x10 -> x0, other arithmetic: 15.9 us -> none  [the longest x2 5.2 us: attend_forward(): row_total = jnp.sum(exponent, -1, keepdims=True)]
  transfers between devices with their start and end apart: 5 -> 0, of which waited for: 4 -> 0; matrix products, arithmetic and copies ran while one was open for 16% -> 0% of each run, Pallas kernels for 0% -> 0%
where the time goes in v2:
time: 189 us
  Pallas kernels  169 us (89%)
  local copies, waits for them, and re-layouts  19 us (10%)
    pallas_call x1, Pallas kernels, layer_call(): pl.pallas_call(partial(layer_kernel, sizes), out_shape=(jax.ShapeDtypeStr...  169 us
    reshape x3, local copies, waits for them, and re-layouts, on_device(): g.reshape(-1)  4.85 us
    unnamed x7, local copies, waits for them, and re-layouts  4.85 us

profile of v2, /device:TPU:0, one launch (start us, length us, event | category | flops | bytes accessed | tf_op | source)
XLA Modules:
  0.0 188.6 jit_solution(8899685077673563207)
XLA Ops:
  0.7 0.7 tile.4
  1.3 0.1 tile.10
  1.4 0.6 pad_bitcast_fusion.vec_in
  2.0 1.4 reshape.50.wo
  3.5 1.7 reshape.49.wq
  5.2 1.6 reshape.51.w1
  6.8 1.7 reshape.52.w2
  8.5 168.8 %shard_map.153 = (bf16[1024,768]{1,0:T(8,128)(2,1)}, bf16[1024,768]{1,0:T(8,128)(2,1)}, f32[24,2304]{1,0:T(8,128)}, f32[24,768]{1,0:T(8,128)}, f32[24,3072]{1,0:...) custom-call(s32[2]{0:T(128)} %lengths.1, s32[2]{0:T(128)} %counts.1, s32[2,128]{1,0:T(2,128)} %positions.1, ...), custom_call_target="tpu_custom_call" | custom-call | tf_op jit(solution)/shard_map/pallas_call | solution.py:677
  177.4 0.0 copy-start.1
  177.4 1.5 dynamic_slice.3
  178.9 1.5 reshape.55
  180.4 1.6 reshape.54
  182.0 1.7 copy.17
  183.7 1.7 reshape.57
  185.4 0.0 copy-done.1
  185.4 0.0 copy-start
  185.4 1.1 copy.20
  186.6 0.8 copy-done
  187.4 1.1 copy.21
  (1 shorter events, 0.0 us)
Async XLA Ops:
  177.4 8.1 %copy-start.1 = (bf16[1024,768]{1,0:T(8,128)(2,1)S(1)}, bf16[1024,768]{1,0:T(8,128)(2,1)}, u32[]{:S(2)}) copy-start(bf16[1024,768]{1,0:T(8,128)(2,1)} %get-tuple-element.28) | copy-start | bytes 4718596
  185.4 2.0 %copy-start = (bf16[1024,768]{1,0:T(8,128)(2,1)S(1)}, bf16[1024,768]{1,0:T(8,128)(2,1)}, u32[]{:S(2)}) copy-start(bf16[1024,768]{1,0:T(8,128)(2,1)} %get-tuple-element.29) | copy-start | bytes 4718596

commit v3 on v2

--- a/solution.py
+++ b/solution.py
@@ -29,34 +29,36 @@
 WIRE = 3 * HALF
 
 gather_types = (
-    "ab", "ab", "ab", "ab", "ab", "e", "f", "e", "f", "e", "f", "ab",
+    "ab", "ab", "ab", "e", "f", "ab", "e", "f", "ab", "e", "f", "ab",
 )
 gather_order = (
-    "0z1", "1z1", "2z1", "11z1", "8s0", "6s0", "10s0", "5s0", "9s0", "7s0", "0z0", "1z0", "3z1",
-    "0B1", "0A1", "2z0", "8z1", "4z1", "1B1", "1A1", "0B2", "0A2", "2B1", "11z0", "1A2", "3z0",
-    "2A1", "1B2", "4z0", "7z1", "6z1", "0C", "2A2", "4B1", "2B2", "3B1", "7z0", "11B1", "3A1",
-    "1C", "11A1", "8z0", "2C", "4A1", "3A2", "6z0", "5z1", "9z1", "3B2", "7s3", "4A2", "10z1",
-    "4B2", "8s3", "5z0", "3C", "9z0", "6s3", "7C", "5s3", "4C", "10z0", "9s3", "8C", "11B2",
-    "10s3", "11A2", "5C", "6C", "9C", "10C", "11C",
+    "0z1", "2z1", "1z1", "3s0", "12v0", "7s0", "11z1", "9s0", "0z0", "10s0", "4s0", "12v1", "6s0",
+    "2z0", "1z0", "5z1", "0B1", "0A1", "11z0", "12v2", "2B1", "2A1", "8z1", "1B1", "1A1", "0B2",
+    "5z0", "10z1", "12v3", "0A2", "8z0", "4z1", "5B1", "11A1", "12v4", "2B2", "5A1", "2A2", "3z1",
+    "9z1", "1A2", "8B1", "0C", "1B2", "6z1", "8A1", "5B2", "4z0", "11B1", "11A2", "3z0", "12v5",
+    "1C", "2C", "10z0", "7z1", "5A2", "4s3", "11B2", "6z0", "3s3", "11C", "7z0", "9z0", "10s3",
+    "6s3", "7s3", "9s3", "5C", "3C", "4C", "8A2", "6C", "8B2", "7C", "9C", "10C", "8C",
 )
 gather_counts = (
-    10, 0, 0, 0, 0, 23, 0, 3, 6, 0, 2, 6, 0, 0, 4, 0, 0, 2, 2, 0, 1, 1, 2, 3, 0, 2, 2, 0, 0, 0, 0,
+    0, 1, 4, 0, 34, 9, 3, 0, 8, 1, 0, 0, 0, 0, 1, 0, 0, 3, 0, 2, 0, 0, 1, 1, 3, 2, 0, 1, 2, 0, 2,
+    0,
 )
 scatter_units = (4, 5, 6, 7, 8, 9, 10, 11, 3, 1, 0, 2)
 scatter_types = (
-    "f", "e", "f", "e", "f", "e", "ab", "ab", "ab", "ab", "ab", "ab",
+    "f", "e", "ab", "f", "e", "ab", "f", "e", "ab", "f", "e", "ab",
 )
 scatter_order = (
-    "0C", "1C", "0s3", "3C", "1s3", "4C", "2C", "4s3", "7C", "3s3", "5C", "7A2", "8C", "6C", "2s3",
-    "0z0", "8B2", "7B2", "5s3", "1z0", "4z0", "8A2", "8B1", "3z0", "9C", "6A2", "0z1", "10C",
-    "11C", "6B2", "11A2", "4z1", "2z0", "11B2", "1z1", "8A1", "3z1", "6B1", "6A1", "5z0", "11B1",
-    "7A1", "11A1", "9A2", "9B2", "8z0", "2z1", "10B2", "6z0", "7B1", "8z1", "11z0", "5z1", "10A2",
-    "7z0", "3s0", "9B1", "11z1", "9A1", "6z1", "10A1", "10B1", "7z1", "4s0", "2s0", "9z0", "5s0",
-    "1s0", "10z0", "0s0", "9z1", "10z1",
+    "0C", "1C", "0s3", "3C", "6C", "1s3", "7C", "4C", "8C", "3s3", "4s3", "0z0", "2C", "5C", "6s3",
+    "1z0", "7s3", "0z1", "2A2", "3z0", "1z1", "2B2", "12v0", "9C", "10C", "6z0", "0s0", "8B2",
+    "4z0", "9s3", "10s3", "11C", "2A1", "8A2", "5A2", "7z0", "11A2", "2B1", "5B2", "4z1", "6z1",
+    "9z0", "12v1", "8B1", "7z1", "11B2", "10z0", "8A1", "5A1", "1s0", "9z1", "11A1", "3z1", "5B1",
+    "11B1", "2z0", "10z1", "8z0", "4s0", "5z0", "6s0", "12v2", "9s0", "11z0", "7s0", "8z1", "12v3",
+    "2z1", "4L", "5z1", "3s0", "10s0", "11z1", "12v4", "1L", "8L", "2L", "10L", "3L", "7L", "6L",
+    "5L", "12v5", "9L", "11L", "0L",
 )
 scatter_counts = (
-    0, 1, 1, 1, 4, 0, 0, 4, 0, 0, 5, 0, 0, 4, 2, 0, 0, 0, 0, 6, 2, 0, 0, 0, 0, 0, 7, 0, 0, 0, 3, 5,
-    3, 2, 1, 5, 1, 3, 2, 6, 2, 1, 1,
+    0, 1, 1, 0, 4, 1, 1, 0, 2, 0, 0, 2, 1, 1, 2, 0, 2, 0, 2, 1, 4, 3, 6, 2, 0, 4, 3, 3, 3, 0, 2, 6,
+    2, 0, 6, 2, 7, 2,
 )
 
 
@@ -158,8 +160,8 @@
 
 
 class Scatter:
-    def __init__(self, place, S, R, send, recv, ready, order):
-        self.place, self.S, self.R = place, S, R
+    def __init__(self, place, S, R, send, recv, ready, order, store):
+        self.place, self.S, self.R, self.store = place, S, R, store
         self.send, self.recv, self.ready = send, recv, ready
         x, y, z0, z1 = place.x, place.y, place.z0, place.z1
         self.legs = {
@@ -187,13 +189,13 @@
         self.got, self.sent = set(), []
         self.turn = {}
         for m, name in order:
-            if "C" in self.leg(m, name)[1] and m not in self.turn:
+            if m < UNITS and "C" in self.leg(m, name)[1] and m not in self.turn:
                 self.turn[m] = len(self.turn)
         self.heard = {b: 0 for b in (X, Y, Z0, Z1)}
 
     def leg(self, m, name):
-        if name == "C":
-            return ("C", (), CORE)
+        if name in "CL":
+            return (name, (), CORE)
         return [leg for leg in self.legs[scatter_types[m]] if leg[0] == name][0]
 
     def copy(self, m, name):
@@ -243,7 +245,7 @@
         self.copy(m, name).start()
         self.sent.append((m, name))
 
-    def last(self, m):
+    def finish(self, m):
         name = self.legs[scatter_types[m]][-1][0]
         self.copy(m, name).wait_recv()
         c = self.place.c
@@ -254,7 +256,7 @@
             jnp.concatenate([v[:, HALF * k : HALF * k + HALF] for v in (left, right)], 1)
             for k in range(3)
         ]
-        return jnp.concatenate(rows, 0)
+        self.store(m, jnp.concatenate(rows, 0))
 
     def drain(self):
         for m, name in self.sent:
@@ -301,14 +303,30 @@
     return u * phi, phi, jnp.exp(-0.5 * u * u) * 0.3989422804014327
 
 
+class Chain:
+    def __init__(self, hop, arrived, size):
+        self.hop, self.arrived, self.size = hop, arrived, size
+
+    def op(self, k):
+        if k > 0:
+            self.arrived(k - 1)
+        if k < self.size:
+            self.hop(k).start()
+
+
 class Schedule:
-    def __init__(self, engine, order, counts):
-        self.engine, self.order, self.counts = engine, list(order), list(counts)
+    def __init__(self, engine, chain, order, counts):
+        self.engine, self.chain, self.order, self.counts = engine, chain, list(order), list(counts)
 
     def run(self, n):
         for _ in range(n):
             m, name = self.order.pop(0)
-            self.engine.op(m, name)
+            if m == UNITS:
+                self.chain.op(int(name[1:]))
+            elif name == "L":
+                self.engine.finish(m)
+            else:
+                self.engine.op(m, name)
 
     def before(self):
         self.run(self.counts.pop(0))
@@ -338,63 +356,71 @@
     lengths, counts, positions, vec_in, wq, wo, w1, w2, x_in, gv_in,
     layer_out, input_grad, g_qkv, g_out, g_up, g_down, g_vec,
     W, S, R, xs, J, ctx_t, act_g, slope_g, pick_t, pick, x_g, q_g, r1_g, n1_g, nl_g, d_two, d_one,
-    f_grad, a_grad, c_grad, dq_g, ctx_gt, acc, n1_t, nl_t, out_t, gv, own_f, oth_f, vec_all, vec, vgrad,
+    f_grad, a_grad, c_grad, dq_g, ctx_gt, acc, n1_t, nl_t, out_t, gv, raw, wide, vec_all, vec, vgrad,
     vsum, vland,
     g_send, g_recv, s_send, s_recv, ready, first, in_sem, out_sem, v_send, v_recv,
 ):
     place = Place(*sizes)
-    c = place.c
-    chip = (place.z1, place.z0, place.y, place.x)
+    c, x, y, z0, z1 = place.bits
+    chip = (z1, z0, y, x)
     load_x = pltpu.make_async_copy(x_in, xs, in_sem.at[0])
+    load_gv = pltpu.make_async_copy(gv_in, gv, in_sem.at[1])
+    weights = ((wq, 0), (wo, 432), (w1, 576), (w2, 1152))
+    own = [
+        pltpu.make_async_copy(w, raw.at[c, at : at + w.shape[0]], in_sem.at[2 + i])
+        for i, (w, at) in enumerate(weights)
+    ]
+    pair = [
+        remote(w, raw.at[c, at : at + w.shape[0]], first.at[2 * i], first.at[2 * i + 1], place.partner(CORE))
+        for i, (w, at) in enumerate(weights)
+    ]
+    for copy in own:
+        copy.start()
     load_x.start()
-    load_gv = pltpu.make_async_copy(gv_in, gv, in_sem.at[1])
     load_gv.start()
+    enter(place)
     G = Gather(place, W, g_send, g_recv)
-    for u, src, at in (
-        [(K_UNIT, wq, D), (V_UNIT, wq, 2 * D), (Q_UNIT, wq, 0), (OUT_UNIT, wo, 0)]
-        + [(UP_UNIT + j, w1, D * j) for j in range(4)]
-    ):
-        own_f[u] = src[:, at : at + D].astype(f32)
-    enter(place)
-    other = pl.ds(pl.multiple_of(HALF * (1 - c), 128), HALF)
-    pair = place.partner(CORE)
-    halves = remote(own_f.at[:, :, other], oth_f, first.at[0], first.at[1], pair)
-    halves.start()
-
-    def vec_hop(b):
-        at = [place.z1, place.z0, place.y, place.x, c]
-        for done in vec_order[: vec_order.index(b)]:
+
+    vec_order = (CORE, X, Y, Z0, Z1)
+
+    def vec_hop(k):
+        at = [z1, z0, y, x, c]
+        for done in vec_order[:k]:
             at[4 - done] = ALL
         part = vec_all.at[tuple(at)]
-        return remote(part, part, v_send.at[b], v_recv.at[b], place.partner(b))
-
-    vec_order = (CORE, X, Y, Z0, Z1)
-    vec_all[tuple(chip) + (c,)] = vec_in[...]
-    vec_hop(CORE).start()
-    downs = []
-    for j in range(2):
-        at = (DOWN_UNIT + 2 * c + j,) + chip
-        down = remote(w2.at[48 * j : 48 * j + 48, other], W.at[at + (ALL, other)], first.at[2 + 2 * j], first.at[3 + 2 * j], pair)
-        down.start()
-        downs.append(down)
-        W[at + (ALL, G.cols)] = w2[48 * j : 48 * j + 48, G.cols]
-    halves.wait_recv()
-    for u in range(8):
-        own, oth = own_f[u, :, G.cols], oth_f[u]
-        low = jnp.where(c == 0, own, oth)
-        high = jnp.where(c == 0, oth, own)
-        W[(u,) + chip + (ALL, G.cols)] = jnp.concatenate([low, high], 0).astype(bf)
-    for down in downs:
-        down.wait_recv()
-    plan = Schedule(G, parse(gather_order), gather_counts)
-    for k in range(5):
+        return remote(part, part, v_send.at[k], v_recv.at[k], place.partner(vec_order[k]))
+
+    pair[0].start()
+    vec_all[chip + (c,)] = vec_in[...]
+    for copy in pair[1:]:
+        copy.start()
+    chain = Chain(vec_hop, lambda k: vec_hop(k).wait_recv(), 5)
+    plan = Schedule(G, chain, parse(gather_order), gather_counts)
+
+    def lay(u, at, stride, n):
+        for j in range(3):
+            col = 3 * c + j
+            if u < DOWN_UNIT:
+                rows = [wide[i, pl.ds(at + col, n, stride=stride), :] for i in range(2)]
+                block = jnp.concatenate(rows, 0)
+            else:
+                block = wide[(u - DOWN_UNIT) // 2, pl.ds(at + col, n, stride=stride), :]
+            W[(u,) + chip + (ALL, pl.ds(pl.multiple_of(128 * col, 128), 128))] = block.astype(bf)
+
+    parts = (
+        [(K_UNIT, 6, 18, ROWS), (V_UNIT, 12, 18, ROWS), (Q_UNIT, 0, 18, ROWS)],
+        [(OUT_UNIT, 432, 6, ROWS)],
+        [(UP_UNIT + j, 576 + 6 * j, 24, ROWS) for j in range(4)],
+        [(DOWN_UNIT + q, 1152 + 6 * 48 * (q % 2), 6, 48) for q in range(4)],
+    )
+    for i, (w, at) in enumerate(weights):
         plan.before()
-        vec_hop(vec_order[k]).wait_recv()
-        if k < 4:
-            vec_hop(vec_order[k + 1]).start()
-    gathered = jnp.sum(vec_all[...].astype(f32).reshape(8, 4, 16, 128), 1)
-    for r in range(72):
-        vec[r // 6 : r // 6 + 1, 128 * (r % 6) : 128 * (r % 6) + 128] = gathered[r // 9, r % 9 : r % 9 + 1]
+        own[i].wait()
+        pair[i].wait_recv()
+        rows = slice(at, at + w.shape[0])
+        wide[:, rows] = raw[:, rows].astype(f32)
+        for part in parts[i]:
+            lay(*part)
 
     def bias(i):
         return vec[pl.ds(i, 1), :]
@@ -406,6 +432,7 @@
         parts = [W[DOWN_UNIT + q, j // 2, j % 2, y, x] for y in range(2) for x in range(2) for q in range(4)]
         return jnp.concatenate(parts, 0)
 
+    plan.before()
     load_x.wait()
     load_gv.wait()
     for s in range(2):
@@ -428,6 +455,10 @@
         plan.loop(2, body)
 
     project(1, K_UNIT, None)
+    plan.before()
+    gathered = jnp.sum(vec_all[...].astype(f32).reshape(8, 4, 16, 128), 1)
+    for r in range(72):
+        vec[r // 6 : r // 6 + 1, 128 * (r % 6) : 128 * (r % 6) + 128] = gathered[r // 9, r % 9 : r % 9 + 1]
     project(2, V_UNIT, 1)
     project(0, Q_UNIT, 0)
 
@@ -499,8 +530,40 @@
     f_grad[...] = two.astype(bf)
     vgrad[9:10, :] = col_sum(f_grad[...])
 
-    T = Scatter(place, S, R, s_send, s_recv, ready, parse(scatter_order))
-    plan = Schedule(T, parse(scatter_order), scatter_counts)
+    def store_unit(m, grad):
+        u = scatter_units[m]
+        if u in (K_UNIT, V_UNIT, Q_UNIT):
+            out, stride, at = g_qkv, 18, 6 * ((u + 1) % 3)
+        elif u == OUT_UNIT:
+            out, stride, at = g_out, 6, 0
+        elif u < DOWN_UNIT:
+            out, stride, at = g_up, 24, 6 * (u - UP_UNIT)
+        else:
+            out, stride, at = g_down, 6, 6 * ROWS * (u - DOWN_UNIT)
+        for j in range(6):
+            out[pl.ds(at + j, ROWS, stride=stride), :] = grad[:, 128 * j : 128 * j + 128]
+
+    hops = [
+        (CORE, (ALL, ALL, ALL), (ALL, ALL, ALL)),
+        (X, (ALL, ALL, ALL), (ALL, ALL, ALL)),
+        (Y, (ALL, ALL, 1 - y), (ALL, ALL, y)),
+        (Z0, (ALL, 1 - z0, y), (ALL, z0, y)),
+        (Z1, (1 - z1, z0, y), (z1, z0, y)),
+    ]
+
+    def hop(k):
+        b, out, _ = hops[k]
+        return remote(vsum.at[out], vland.at[(k,) + out], v_send.at[5 + k], v_recv.at[5 + k], place.partner(b))
+
+    def hop_arrived(k):
+        copy = hop(k)
+        copy.wait_send()
+        copy.wait_recv()
+        own = hops[k][2]
+        vsum[own] = vsum[own] + vland[(k,) + own]
+
+    T = Scatter(place, S, R, s_send, s_recv, ready, parse(scatter_order), store_unit)
+    plan = Schedule(T, Chain(hop, hop_arrived, 5), parse(scatter_order), scatter_counts)
     message = {u: m for m, u in enumerate(scatter_units)}
 
     def put(m, grad):
@@ -572,31 +635,6 @@
 
     for r in range(72):
         vsum[r // 36, r // 18 % 2, r // 9 % 2, r % 9 : r % 9 + 1] = vgrad[r // 6 : r // 6 + 1, 128 * (r % 6) : 128 * (r % 6) + 128]
-    y, z0, z1 = place.y, place.z0, place.z1
-    hops = [
-        (CORE, (ALL, ALL, ALL), (ALL, ALL, ALL)),
-        (X, (ALL, ALL, ALL), (ALL, ALL, ALL)),
-        (Y, (ALL, ALL, 1 - y), (ALL, ALL, y)),
-        (Z0, (ALL, 1 - z0, y), (ALL, z0, y)),
-        (Z1, (1 - z1, z0, y), (z1, z0, y)),
-    ]
-
-    def hop(k):
-        b, out, _ = hops[k]
-        return remote(vsum.at[out], vland.at[(k,) + out], v_send.at[5 + k], v_recv.at[5 + k], place.partner(b))
-
-    def take(k):
-        copy = hop(k)
-        copy.wait_send()
-        copy.wait_recv()
-        own = hops[k][2]
-        vsum[own] = vsum[own] + vland[(k,) + own]
-
-    for k in range(5):
-        plan.before()
-        if k > 0:
-            take(k - 1)
-        hop(k).start()
 
     def ffn_all(it):
         t, q = it // 4, it % 4
@@ -625,8 +663,6 @@
             done.start()
 
     plan.loop(16, ffn_all)
-    take(4)
-    g_vec[...] = vsum[z1, z0, y]
 
     def grad_in(s):
         rows = pl.ds(pl.multiple_of(s * SEQ_LEN, SEQ_LEN), SEQ_LEN)
@@ -643,26 +679,13 @@
     store = pltpu.make_async_copy(J.at[0], input_grad, out_sem.at[1])
     store.start()
     plan.rest()
-    for m, u in enumerate(scatter_units):
-        grad = T.last(m)
-        if u in (K_UNIT, V_UNIT, Q_UNIT):
-            at = D * ((u + 1) % 3)
-            g_qkv[:, at : at + D] = grad
-        elif u == OUT_UNIT:
-            g_out[...] = grad
-        elif u < DOWN_UNIT:
-            at = D * (u - UP_UNIT)
-            g_up[:, at : at + D] = grad
-        else:
-            at = ROWS * (u - DOWN_UNIT)
-            g_down[at : at + ROWS, :] = grad
+    g_vec[...] = vsum[z1, z0, y]
     pltpu.make_async_copy(out_t, layer_out.at[0:256, :], out_sem.at[0]).wait()
     store.wait()
-    halves.wait_send()
-    for down in downs:
-        down.wait_send()
-    for b in vec_order:
-        vec_hop(b).wait_send()
+    for copy in pair:
+        copy.wait_send()
+    for k in range(5):
+        vec_hop(k).wait_send()
     G.drain()
     T.drain()
 
@@ -679,13 +702,13 @@
         out_shape=(
             jax.ShapeDtypeStruct((tokens, D), bf),
             jax.ShapeDtypeStruct((tokens, D), bf),
-            jax.ShapeDtypeStruct((ROWS, 3 * D), f32),
-            jax.ShapeDtypeStruct((ROWS, D), f32),
-            jax.ShapeDtypeStruct((ROWS, FF), f32),
-            jax.ShapeDtypeStruct((FF // PARTS, D), f32),
+            jax.ShapeDtypeStruct((432, 128), f32),
+            jax.ShapeDtypeStruct((144, 128), f32),
+            jax.ShapeDtypeStruct((576, 128), f32),
+            jax.ShapeDtypeStruct((576, 128), f32),
             jax.ShapeDtypeStruct((16, 128), f32),
         ),
-        in_specs=[smem, smem] + [vmem] * 6 + [hbm] * 2,
+        in_specs=[smem, smem] + [vmem] * 2 + [hbm] * 6,
         out_specs=(hbm,) * 2 + (vmem,) * 5,
         scratch_shapes=[
             pltpu.VMEM((UNITS, 2, 2, 2, 2, 2 * ROWS, D), bf),
@@ -715,8 +738,8 @@
             pltpu.VMEM((256, D), bf),
             pltpu.VMEM((256, D), bf),
             pltpu.VMEM((slots, D), bf),
-            pltpu.VMEM((8, ROWS, D), f32),
-            pltpu.VMEM((8, ROWS, HALF), f32),
+            pltpu.VMEM((2, 1728, 128), bf),
+            pltpu.VMEM((2, 1728, 128), f32),
             pltpu.VMEM((2, 2, 2, 2, 2, 16, 128), bf),
             pltpu.VMEM((16, D), f32),
             pltpu.VMEM((16, D), f32),
@@ -727,8 +750,8 @@
             dma((UNITS, 7)),
             dma((UNITS, 7)),
             pltpu.SemaphoreType.REGULAR((4,)),
+            dma((8,)),
             dma((6,)),
-            dma((2,)),
             dma((2,)),
             dma((10,)),
             dma((10,)),
@@ -737,6 +760,33 @@
             collective_id=0, has_side_effects=True, vmem_limit_bytes=63 * 2**20
         ),
     )(*args)
+
+
+def settle_kernel(n, *refs):
+    ins, outs, held, sems = refs[:n], refs[n : 2 * n], refs[2 * n : 3 * n], refs[-1]
+    loads = [pltpu.make_async_copy(ins[i], held[i], sems.at[i]) for i in range(n)]
+    stores = [pltpu.make_async_copy(held[i], outs[i], sems.at[n + i]) for i in range(n)]
+    for load in loads:
+        load.start()
+    for load, store in zip(loads, stores):
+        load.wait()
+        store.start()
+    for store in stores:
+        store.wait()
+
+
+def settle(*arrays):
+    hbm = pl.BlockSpec(memory_space=pltpu.HBM)
+    n = len(arrays)
+    return pl.pallas_call(
+        partial(settle_kernel, n),
+        out_shape=[jax.ShapeDtypeStruct(a.shape, a.dtype) for a in arrays],
+        in_specs=[pl.BlockSpec(memory_space=pl.ANY)] * n,
+        out_specs=[hbm] * n,
+        scratch_shapes=[pltpu.VMEM(a.shape, a.dtype) for a in arrays]
+        + [pltpu.SemaphoreType.DMA((2 * n,))],
+        compiler_params=pltpu.CompilerParams(vmem_limit_bytes=63 * 2**20),
+    )(*arrays)
 
 
 def sub_groups(sizes):
@@ -777,22 +827,24 @@
     number = lax.axis_index("dp") * sizes[1] + lax.axis_index("inner")
     quarter = number // (sizes[0] * sizes[1] // PARTS) % 4
     size = vec.shape[0]
-    frame = jnp.where(jnp.arange(4 * size) // size == quarter, jnp.tile(vec, 4), bf(0))
-    frame = jnp.pad(frame, (0, 16 * 128 - 4 * size)).reshape(16, 128)
+    frame = lax.dynamic_update_slice(jnp.zeros((16 * 128,), bf), vec, (quarter * size,)).reshape(16, 128)
     layer_out, input_grad, g_qkv, g_out, g_up, g_down, g_vec = layer_call(
         sizes,
         lengths,
         counts,
         positions,
         frame,
-        wq.reshape(ROWS, 3 * D),
-        wo.reshape(ROWS, D),
-        w1.reshape(ROWS, FF),
-        w2.reshape(FF // PARTS, D),
+        wq.reshape(-1, 128),
+        wo.reshape(-1, 128),
+        w1.reshape(-1, 128),
+        w2.reshape(-1, 128),
         inputs,
         grad_values.reshape(-1, D),
     )
     g_vec = lax.dynamic_slice(g_vec.reshape(-1), (quarter * size,), (size,))
+    layer_out, input_grad, g_qkv, g_out, g_up, g_down = settle(
+        layer_out, input_grad, g_qkv, g_out, g_up, g_down
+    )
     flat = [own_part(sizes, g.reshape(-1)) for g in (g_qkv, g_out, g_up, g_down, g_vec)]
     return (layer_out, input_grad, *flat)
 

time: 189 us -> 159 us (0.84)
  local copies, waits for them, and re-layouts: 19 us -> 2.83 us
  Pallas kernels: 169 us -> 155 us
    pallas_call x1, Pallas kernels: 169 us -> 152 us  [layer_call(): pl.pallas_call(partial(layer_kernel, sizes), out_shape=(jax.ShapeDtypeStr...]
    reshape x8 -> x0, local copies, waits for them, and re-layouts: 11.9 us -> none  [the longest x3 4.85 us: on_device(): g.reshape(-1)]
    unnamed x7 -> x2, local copies, waits for them, and re-layouts: 4.85 us -> 0.59 us
    pallas_call x0 -> x1, Pallas kernels: none -> 3.46 us  [settle(): pl.pallas_call(partial(settle_kernel, n), out_shape=[jax.ShapeDtypeStruct...]
where the time goes in v3:
time: 159 us
  Pallas kernels  155 us (97%)
  local copies, waits for them, and re-layouts  2.83 us (2%)
    pallas_call x1, Pallas kernels, layer_call(): pl.pallas_call(partial(layer_kernel, sizes), out_shape=(jax.ShapeDtypeStr...  152 us
    pallas_call x1, Pallas kernels, settle(): pl.pallas_call(partial(settle_kernel, n), out_shape=[jax.ShapeDtypeStruct...  3.46 us

profile of v3, /device:TPU:0, one launch (start us, length us, event | category | flops | bytes accessed | tf_op | source)
XLA Modules:
  0.0 159.0 jit_solution(4983723107196697685)
XLA Ops:
  0.7 0.9 dynamic_update_slice.3
  1.5 0.0 copy-start
  1.5 0.6 copy-done
  2.1 152.0 %shard_map.153 = (bf16[1024,768]{1,0:T(8,128)(2,1)}, bf16[1024,768]{1,0:T(8,128)(2,1)}, f32[432,128]{1,0:T(8,128)}, f32[144,128]{1,0:T(8,128)}, f32[576,128]{1,0...) custom-call(s32[2]{0:T(128)} %lengths.1, s32[2]{0:T(128)} %counts.1, s32[2,128]{1,0:T(2,128)} %positions.1, ...), custom_call_target="tpu_custom_call" | custom-call | tf_op jit(solution)/shard_map/pallas_call | solution.py:700
  154.2 3.5 %shard_map.154 = (bf16[1024,768]{1,0:T(8,128)(2,1)}, bf16[1024,768]{1,0:T(8,128)(2,1)}, f32[432,128]{1,0:T(8,128)}, f32[144,128]{1,0:T(8,128)}, f32[576,128]{1,0:T(8,128)}, /*index=5*/f32[576,128]{1,0:T(8,128)}) custom-call(bf16[1024,768]{1,0:T(8,128)(2,1)} %get-tuple-element.20.refs_0_, bf16[1024,768]{1,0:T(8,128)(2,1)} %get-tuple-element.21.refs_1_, ...), custom_call_target="tpu_custom_call" | custom-call | tf_op jit(solution)/shard_map/pallas_call | solution.py:781
  157.6 1.4 dynamic_slice.3
  (1 shorter events, 0.0 us)
Async XLA Ops:
  1.5 0.6 copy-start

commit v4 on v3

--- a/solution.py
+++ b/solution.py
@@ -29,36 +29,37 @@
 WIRE = 3 * HALF
 
 gather_types = (
-    "ab", "ab", "ab", "e", "f", "ab", "e", "f", "ab", "e", "f", "ab",
+    "ab", "ab", "ab", "ab", "ab", "gx", "gx", "ab", "ab", "ab", "ab", "gy",
 )
 gather_order = (
-    "0z1", "2z1", "1z1", "3s0", "12v0", "7s0", "11z1", "9s0", "0z0", "10s0", "4s0", "12v1", "6s0",
-    "2z0", "1z0", "5z1", "0B1", "0A1", "11z0", "12v2", "2B1", "2A1", "8z1", "1B1", "1A1", "0B2",
-    "5z0", "10z1", "12v3", "0A2", "8z0", "4z1", "5B1", "11A1", "12v4", "2B2", "5A1", "2A2", "3z1",
-    "9z1", "1A2", "8B1", "0C", "1B2", "6z1", "8A1", "5B2", "4z0", "11B1", "11A2", "3z0", "12v5",
-    "1C", "2C", "10z0", "7z1", "5A2", "4s3", "11B2", "6z0", "3s3", "11C", "7z0", "9z0", "10s3",
-    "6s3", "7s3", "9s3", "5C", "3C", "4C", "8A2", "6C", "8B2", "7C", "9C", "10C", "8C",
+    "1z1", "12v0", "0z1", "5s0", "12v1", "2z1", "6s0", "9z1", "11s0", "1z0", "5s1", "12v2", "11s1",
+    "6s1", "0z0", "2z0", "1A1", "1B1", "0A1", "9z0", "0B1", "12v3", "8z1", "4z1", "10z1", "2A1",
+    "2B1", "0B2", "7z1", "0A2", "3z1", "4z0", "8z0", "12v4", "1A2", "1B2", "0C", "3z0", "2B2",
+    "7z0", "5z1", "2A2", "10z0", "4B1", "8B1", "4A1", "12v5", "1C", "3B1", "3A1", "8A1", "6z1",
+    "9A1", "2C", "9B1", "7B1", "4B2", "4A2", "11z1", "10A1", "8A2", "10B1", "5z0", "7A1", "3A2",
+    "6z0", "3B2", "9A2", "8B2", "4C", "9B2", "7A2", "7B2", "10A2", "3C", "10B2", "11z0", "5C",
+    "6C", "9C", "7C", "8C", "10C", "11C",
 )
 gather_counts = (
-    0, 1, 4, 0, 34, 9, 3, 0, 8, 1, 0, 0, 0, 0, 1, 0, 0, 3, 0, 2, 0, 0, 1, 1, 3, 2, 0, 1, 2, 0, 2,
-    0,
+    0, 2, 1, 4, 35, 0, 4, 5, 3, 2, 0, 2, 2, 0, 0, 0, 4, 3, 3, 1, 0, 1, 1, 0, 0, 4, 0, 2, 1, 1, 1,
+    2,
 )
 scatter_units = (4, 5, 6, 7, 8, 9, 10, 11, 3, 1, 0, 2)
 scatter_types = (
-    "f", "e", "ab", "f", "e", "ab", "f", "e", "ab", "f", "e", "ab",
+    "gx", "ab", "gy", "ab", "gx", "ab", "ab", "ab", "ab", "ab", "ab", "ab",
 )
 scatter_order = (
-    "0C", "1C", "0s3", "3C", "6C", "1s3", "7C", "4C", "8C", "3s3", "4s3", "0z0", "2C", "5C", "6s3",
-    "1z0", "7s3", "0z1", "2A2", "3z0", "1z1", "2B2", "12v0", "9C", "10C", "6z0", "0s0", "8B2",
-    "4z0", "9s3", "10s3", "11C", "2A1", "8A2", "5A2", "7z0", "11A2", "2B1", "5B2", "4z1", "6z1",
-    "9z0", "12v1", "8B1", "7z1", "11B2", "10z0", "8A1", "5A1", "1s0", "9z1", "11A1", "3z1", "5B1",
-    "11B1", "2z0", "10z1", "8z0", "4s0", "5z0", "6s0", "12v2", "9s0", "11z0", "7s0", "8z1", "12v3",
-    "2z1", "4L", "5z1", "3s0", "10s0", "11z1", "12v4", "1L", "8L", "2L", "10L", "3L", "7L", "6L",
-    "5L", "12v5", "9L", "11L", "0L",
+    "0C", "1C", "3C", "2C", "0z0", "1B2", "1A2", "3B2", "6C", "3A2", "5C", "2z0", "1A1", "7C",
+    "6A2", "4C", "6B2", "8C", "1B1", "0z1", "7A2", "7B2", "8A2", "5B2", "4z0", "3B1", "6A1", "8B2",
+    "2z1", "5A2", "3A1", "9C", "7A1", "7B1", "12v0", "4z1", "12v1", "5B1", "6B1", "10C", "9A2",
+    "8A1", "5A1", "3z0", "7z0", "8B1", "11C", "10B2", "1z0", "9B2", "10A2", "12v2", "5z0", "3z1",
+    "9A1", "6z0", "11A2", "9B1", "11B2", "8z0", "5z1", "10B1", "1z1", "10A1", "6z1", "12v3", "2s1",
+    "11B1", "4s1", "9z0", "8z1", "11A1", "0s1", "7z1", "12v4", "10z0", "11z0", "2s0", "9z1", "0s0",
+    "6L", "10z1", "4s0", "11z1", "3L", "2L", "0L", "9L", "1L", "5L", "7L", "12v5", "8L", "4L",
+    "10L", "11L",
 )
 scatter_counts = (
-    0, 1, 1, 0, 4, 1, 1, 0, 2, 0, 0, 2, 1, 1, 2, 0, 2, 0, 2, 1, 4, 3, 6, 2, 0, 4, 3, 3, 3, 0, 2, 6,
-    2, 0, 6, 2, 7, 2,
+    0, 1, 1, 0, 1, 4, 0, 1, 2, 9, 1, 2, 2, 1, 1, 2, 2, 4, 1, 8, 5, 4, 4, 5, 5, 8, 2, 7,
 )
 
 
@@ -102,8 +103,8 @@
 
 
 class Gather:
-    def __init__(self, place, W, send, recv):
-        self.place, self.W, self.send, self.recv = place, W, send, recv
+    def __init__(self, place, W, V, send, recv):
+        self.place, self.W, self.V, self.send, self.recv = place, W, V, send, recv
         self.cols = pl.ds(pl.multiple_of(HALF * place.c, 128), HALF)
         x, y, z0, z1 = place.x, place.y, place.z0, place.z1
         every = (ALL, ALL, ALL, ALL)
@@ -131,6 +132,20 @@
                 ("s3", ("z0",), X, (ALL, ALL, ALL, x)),
                 ("C", ("s3",), CORE, every),
             ],
+            "gx": [
+                ("s0", (), X, (z1, z0, y, x)),
+                ("s1", ("s0",), Y, (z1, z0, y, ALL)),
+                ("z1", ("s1",), Z1, (z1, z0, ALL, ALL)),
+                ("z0", ("z1",), Z0, (ALL, z0, ALL, ALL)),
+                ("C", ("z0",), CORE, every),
+            ],
+            "gy": [
+                ("s0", (), Y, (z1, z0, y, x)),
+                ("s1", ("s0",), X, (z1, z0, ALL, x)),
+                ("z1", ("s1",), Z1, (z1, z0, ALL, ALL)),
+                ("z0", ("z1",), Z0, (ALL, z0, ALL, ALL)),
+                ("C", ("z0",), CORE, every),
+            ],
         }
         self.got, self.sent = set(), []
 
@@ -138,7 +153,10 @@
         legs = self.legs[gather_types[m]]
         k = [leg[0] for leg in legs].index(name)
         _, after, b, index = legs[k]
-        part = self.W.at[(m,) + index + (ALL, self.cols)]
+        if m < DOWN_UNIT:
+            part = self.W.at[(m,) + index + (ALL, self.cols)]
+        else:
+            part = self.V.at[index + (m - DOWN_UNIT, ALL, self.cols)]
         sems = self.send.at[m, k], self.recv.at[m, k]
         return remote(part, part, *sems, self.place.partner(b)), after
 
@@ -160,8 +178,8 @@
 
 
 class Scatter:
-    def __init__(self, place, S, R, send, recv, ready, order, store):
-        self.place, self.S, self.R, self.store = place, S, R, store
+    def __init__(self, place, S, R, N, send, recv, ready, order, store):
+        self.place, self.S, self.R, self.N, self.store = place, S, R, N, store
         self.send, self.recv, self.ready = send, recv, ready
         x, y, z0, z1 = place.x, place.y, place.z0, place.z1
         self.legs = {
@@ -185,6 +203,18 @@
                 ("z1", ("z0",), Z1, (1 - z1, z0, ALL, x), (1 - z1, 1 - z0, ALL, 1 - x), (z1, z0, ALL, x), (z1, 1 - z0, ALL, 1 - x)),
                 ("s0", ("z1",), Y, (z1, z0, 1 - y, x), (1 - z1, 1 - z0, 1 - y, 1 - x), (z1, z0, y, x), (1 - z1, 1 - z0, y, 1 - x)),
             ],
+            "gx": [
+                ("z0", ("C",), Z0, (ALL, 1 - z0, ALL, ALL), (ALL, 1 - z0, ALL, ALL), (ALL, z0, ALL, ALL), (ALL, z0, ALL, ALL)),
+                ("z1", ("z0",), Z1, (1 - z1, z0, ALL, ALL), (1 - z1, 1 - z0, ALL, ALL), (z1, z0, ALL, ALL), (z1, 1 - z0, ALL, ALL)),
+                ("s1", ("z1",), Y, (z1, z0, 1 - y, ALL), (1 - z1, 1 - z0, 1 - y, ALL), (z1, z0, y, ALL), (1 - z1, 1 - z0, y, ALL)),
+                ("s0", ("s1",), X, (z1, z0, y, 1 - x), (1 - z1, 1 - z0, 1 - y, 1 - x), (z1, z0, y, x), (1 - z1, 1 - z0, 1 - y, x)),
+            ],
+            "gy": [
+                ("z0", ("C",), Z0, (ALL, 1 - z0, ALL, ALL), (ALL, 1 - z0, ALL, ALL), (ALL, z0, ALL, ALL), (ALL, z0, ALL, ALL)),
+                ("z1", ("z0",), Z1, (1 - z1, z0, ALL, ALL), (1 - z1, 1 - z0, ALL, ALL), (z1, z0, ALL, ALL), (z1, 1 - z0, ALL, ALL)),
+                ("s1", ("z1",), X, (z1, z0, ALL, 1 - x), (1 - z1, 1 - z0, ALL, 1 - x), (z1, z0, ALL, x), (1 - z1, 1 - z0, ALL, x)),
+                ("s0", ("s1",), Y, (z1, z0, 1 - y, x), (1 - z1, 1 - z0, 1 - y, 1 - x), (z1, z0, y, x), (1 - z1, 1 - z0, y, 1 - x)),
+            ],
         }
         self.got, self.sent = set(), []
         self.turn = {}
@@ -204,11 +234,13 @@
             sems = self.send.at[m, 0], self.recv.at[m, 0]
             return remote(self.S.at[m, 1 - c], self.R.at[m], *sems, self.place.partner(CORE))
         k = [leg[0] for leg in self.legs[scatter_types[m]]].index(name) + 1
-        _, _, b, out, land, _, _ = self.leg(m, name)
+        _, after, b, out, land, _, _ = self.leg(m, name)
         sems = self.send.at[m, k], self.recv.at[m, k]
-        return remote(
-            self.S.at[(m, c) + out], self.S.at[(m, 1 - c) + land], *sems, self.place.partner(b)
-        )
+        there = self.N.at[self.early(m, name)] if "C" in after else self.S.at[(m, 1 - c) + land]
+        return remote(self.S.at[(m, c) + out], there, *sems, self.place.partner(b))
+
+    def early(self, m, name):
+        return {"A2": (m, 0), "B2": (m, 1)}.get(name, (m,))
 
     def add(self, m, name):
         if (m, name) in self.got:
@@ -230,14 +262,15 @@
             self.S[m, c] = self.S[m, c] + self.R[m]
             return
         copy.wait_recv()
-        own, landed = self.leg(m, name)[5:]
-        self.S[(m, c) + own] = self.S[(m, c) + own] + self.S[(m, 1 - c) + landed]
+        _, after, _, _, _, own, landed = self.leg(m, name)
+        came = self.N[self.early(m, name)] if "C" in after else self.S[(m, 1 - c) + landed]
+        self.S[(m, c) + own] = self.S[(m, c) + own] + came
 
     def op(self, m, name):
         after, b = self.leg(m, name)[1:3]
         for a in after:
             self.add(m, a)
-        if b != CORE:
+        if b != CORE and "C" not in after:
             need = self.turn[m] + 1 - self.heard[b]
             if need > 0:
                 pl.semaphore_wait(self.ready.at[b - 1], need)
@@ -298,9 +331,12 @@
     return jnp.sum(rows.astype(f32), 0, keepdims=True)
 
 
-def gelu_parts(u):
-    phi = 0.5 + 0.5 * lax.erf(u * 0.7071067811865476)
-    return u * phi, phi, jnp.exp(-0.5 * u * u) * 0.3989422804014327
+def normal_cdf(u):
+    return 0.5 + 0.5 * lax.erf(u * 0.7071067811865476)
+
+
+def normal_density(u):
+    return jnp.exp(-0.5 * u * u) * 0.3989422804014327
 
 
 class Chain:
@@ -355,8 +391,8 @@
     sizes,
     lengths, counts, positions, vec_in, wq, wo, w1, w2, x_in, gv_in,
     layer_out, input_grad, g_qkv, g_out, g_up, g_down, g_vec,
-    W, S, R, xs, J, ctx_t, act_g, slope_g, pick_t, pick, x_g, q_g, r1_g, n1_g, nl_g, d_two, d_one,
-    f_grad, a_grad, c_grad, dq_g, ctx_gt, acc, n1_t, nl_t, out_t, gv, raw, wide, vec_all, vec, vgrad,
+    W, V, S, R, N, xs, J, ctx_t, act_g, slope_g, pick_t, x_g, q_g, res_g, acc_g, nl_g,
+    f_grad, dq_g, ctx_gt, acc, nl_t, out_t, wide, vec_all, vec, vgrad,
     vsum, vland,
     g_send, g_recv, s_send, s_recv, ready, first, in_sem, out_sem, v_send, v_recv,
 ):
@@ -364,22 +400,27 @@
     c, x, y, z0, z1 = place.bits
     chip = (z1, z0, y, x)
     load_x = pltpu.make_async_copy(x_in, xs, in_sem.at[0])
-    load_gv = pltpu.make_async_copy(gv_in, gv, in_sem.at[1])
-    weights = ((wq, 0), (wo, 432), (w1, 576), (w2, 1152))
+    load_gv = pltpu.make_async_copy(gv_in, dq_g, in_sem.at[1])
+    weights = ((wq, 0, 0), (wo, 0, 432), (w1, 1, 0), (w2, 2, 0))
+
+    def flat_part(w, block, at):
+        cols = pl.ds(pl.multiple_of(HALF * c + 128 * block, 128), 128)
+        return out_t.at[at : at + w.shape[0], cols]
+
     own = [
-        pltpu.make_async_copy(w, raw.at[c, at : at + w.shape[0]], in_sem.at[2 + i])
-        for i, (w, at) in enumerate(weights)
+        pltpu.make_async_copy(w, flat_part(w, block, at), in_sem.at[2 + i])
+        for i, (w, block, at) in enumerate(weights)
     ]
     pair = [
-        remote(w, raw.at[c, at : at + w.shape[0]], first.at[2 * i], first.at[2 * i + 1], place.partner(CORE))
-        for i, (w, at) in enumerate(weights)
+        remote(w, flat_part(w, block, at), first.at[2 * i], first.at[2 * i + 1], place.partner(CORE))
+        for i, (w, block, at) in enumerate(weights)
     ]
     for copy in own:
         copy.start()
     load_x.start()
     load_gv.start()
     enter(place)
-    G = Gather(place, W, g_send, g_recv)
+    G = Gather(place, W, V, g_send, g_recv)
 
     vec_order = (CORE, X, Y, Z0, Z1)
 
@@ -405,20 +446,26 @@
                 block = jnp.concatenate(rows, 0)
             else:
                 block = wide[(u - DOWN_UNIT) // 2, pl.ds(at + col, n, stride=stride), :]
-            W[(u,) + chip + (ALL, pl.ds(pl.multiple_of(128 * col, 128), 128))] = block.astype(bf)
+            cols = pl.ds(pl.multiple_of(128 * col, 128), 128)
+            if u < DOWN_UNIT:
+                W[(u,) + chip + (ALL, cols)] = block.astype(bf)
+            else:
+                V[chip + (u - DOWN_UNIT, ALL, cols)] = block.astype(bf)
 
     parts = (
         [(K_UNIT, 6, 18, ROWS), (V_UNIT, 12, 18, ROWS), (Q_UNIT, 0, 18, ROWS)],
-        [(OUT_UNIT, 432, 6, ROWS)],
-        [(UP_UNIT + j, 576 + 6 * j, 24, ROWS) for j in range(4)],
-        [(DOWN_UNIT + q, 1152 + 6 * 48 * (q % 2), 6, 48) for q in range(4)],
+        [(OUT_UNIT, 0, 6, ROWS)],
+        [(UP_UNIT + j, 6 * j, 24, ROWS) for j in range(4)],
+        [(DOWN_UNIT + q, 6 * 48 * (q % 2), 6, 48) for q in range(4)],
     )
-    for i, (w, at) in enumerate(weights):
+    for i, (w, block, at) in enumerate(weights):
         plan.before()
         own[i].wait()
         pair[i].wait_recv()
-        rows = slice(at, at + w.shape[0])
-        wide[:, rows] = raw[:, rows].astype(f32)
+        n = w.shape[0]
+        for k in range(2):
+            col = HALF * k + 128 * block
+            wide[k, :n] = out_t[at : at + n, col : col + 128].astype(f32)
         for part in parts[i]:
             lay(*part)
 
@@ -429,8 +476,7 @@
         return W[u].reshape(D, D)
 
     def down_block(j):
-        parts = [W[DOWN_UNIT + q, j // 2, j % 2, y, x] for y in range(2) for x in range(2) for q in range(4)]
-        return jnp.concatenate(parts, 0)
+        return V[j // 2, j % 2].reshape(D, D)
 
     plan.before()
     load_x.wait()
@@ -441,8 +487,7 @@
         match = (positions[s : s + 1, :] == place_id) & (slot_id < counts[s])
         hot = jnp.where(match, 1.0, 0.0)
         pick_t[s] = hot.astype(bf)
-        pick[s] = hot.T.astype(bf)
-        x_g[PMAX * s : PMAX * s + PMAX] = dot(pick[s], xs[SEQ_LEN * s : SEQ_LEN * s + SEQ_LEN], 1, 0).astype(bf)
+        x_g[PMAX * s : PMAX * s + PMAX] = dot(pick_t[s], xs[SEQ_LEN * s : SEQ_LEN * s + SEQ_LEN], 0, 0).astype(bf)
 
     def project(i, u, b):
         def body(t):
@@ -493,40 +538,38 @@
     for s in range(2):
         rows = slice(SEQ_LEN * s, SEQ_LEN * s + SEQ_LEN)
         slots = slice(PMAX * s, PMAX * s + PMAX)
-        ctx_gt[:, slots] = dot(ctx_t[:, rows], pick[s], 1, 1).astype(bf)
-        q_g[slots, :] = dot(pick[s], J[0, rows, :], 1, 0).astype(bf)
+        ctx_gt[:, slots] = dot(ctx_t[:, rows], pick_t[s], 1, 0).astype(bf)
+        q_g[slots, :] = dot(pick_t[s], J[0, rows, :], 0, 0).astype(bf)
     r1 = x_g[...].astype(f32) + (dot(ctx_gt[...], unit(OUT_UNIT), 0, 0) + bias(2))
-    r1_g[...] = r1
+    res_g[...] = r1
     n1 = norm(r1)[0] * bias(3) + bias(4)
-    n1_g[...] = n1
+    acc_g[...] = n1 + bias(9)
     nl_g[...] = n1.astype(bf)
 
     def up_listed(q):
         cols = pl.ds(pl.multiple_of(D * q, D), D)
         u = dot(nl_g[...], unit(UP_UNIT + q), 1, 0) + bias(5 + q)
-        a, phi, density = gelu_parts(u)
-        act_g[:, cols] = a.astype(bf)
-        slope_g[:, cols] = (phi + u * density).astype(bf)
+        phi = normal_cdf(u)
+        act_g[:, cols] = (u * phi).astype(bf)
+        slope_g[:, cols] = (phi + u * normal_density(u)).astype(bf)
 
     plan.loop(4, up_listed, lambda q: G.arrive(UP_UNIT + q))
     plan.rest()
     for u in range(DOWN_UNIT, UNITS):
         G.arrive(u)
 
-    acc[...] = n1_g[...] + bias(9)
-
     @pl.loop(0, 4)
     def _(q):
         cols = pl.ds(pl.multiple_of(D * q, D), D)
-        acc[...] += dot(act_g[:, cols], down_block(q), 1, 0)
-
-    rhat, rstd = norm(acc[...])
-    used = [jnp.sum(pick[s].astype(f32), 1, keepdims=True) for s in range(2)]
-    cot = jnp.where(jnp.concatenate(used, 0) > 0.5, gv[...].astype(f32), 0.0)
+        acc_g[...] += dot(act_g[:, cols], down_block(q), 1, 0)
+
+    rhat, rstd = norm(acc_g[...])
+    used = [dot(pick_t[s], jnp.ones((SEQ_LEN, 128), bf), 0, 0)[:, :1] for s in range(2)]
+    cot = jnp.where(jnp.concatenate(used, 0) > 0.5, dq_g[...].astype(f32), 0.0)
     vgrad[10:11, :] = col_sum(cot * rhat)
     vgrad[11:12, :] = col_sum(cot)
     two = norm_back(cot * bias(10), rhat, rstd)
-    d_two[...] = two
+    acc_g[...] = two
     f_grad[...] = two.astype(bf)
     vgrad[9:10, :] = col_sum(f_grad[...])
 
@@ -543,26 +586,27 @@
         for j in range(6):
             out[pl.ds(at + j, ROWS, stride=stride), :] = grad[:, 128 * j : 128 * j + 128]
 
+    whole = (ALL, ALL, ALL)
     hops = [
-        (CORE, (ALL, ALL, ALL), (ALL, ALL, ALL)),
-        (X, (ALL, ALL, ALL), (ALL, ALL, ALL)),
-        (Y, (ALL, ALL, 1 - y), (ALL, ALL, y)),
-        (Z0, (ALL, 1 - z0, y), (ALL, z0, y)),
-        (Z1, (1 - z1, z0, y), (z1, z0, y)),
+        (CORE, whole, (0,) + whole, whole, (0,) + whole),
+        (X, whole, (1,) + whole, whole, (1,) + whole),
+        (Y, (ALL, ALL, 1 - y), (2, ALL, ALL, 1 - y), (ALL, ALL, y), (2, ALL, ALL, y)),
+        (Z0, (ALL, 1 - z0, y), (2, ALL, 1 - z0, 1 - y), (ALL, z0, y), (2, ALL, z0, 1 - y)),
+        (Z1, (1 - z1, z0, y), (2, 1 - z1, 1 - z0, 1 - y), (z1, z0, y), (2, z1, 1 - z0, 1 - y)),
     ]
 
     def hop(k):
-        b, out, _ = hops[k]
-        return remote(vsum.at[out], vland.at[(k,) + out], v_send.at[5 + k], v_recv.at[5 + k], place.partner(b))
+        b, out, land, _, _ = hops[k]
+        return remote(vsum.at[out], vland.at[land], v_send.at[5 + k], v_recv.at[5 + k], place.partner(b))
 
     def hop_arrived(k):
         copy = hop(k)
         copy.wait_send()
         copy.wait_recv()
-        own = hops[k][2]
-        vsum[own] = vsum[own] + vland[(k,) + own]
-
-    T = Scatter(place, S, R, s_send, s_recv, ready, parse(scatter_order), store_unit)
+        own, landed = hops[k][3:]
+        vsum[own] = vsum[own] + vland[landed]
+
+    T = Scatter(place, S, R, N, s_send, s_recv, ready, parse(scatter_order), store_unit)
     plan = Schedule(T, Chain(hop, hop_arrived, 5), parse(scatter_order), scatter_counts)
     message = {u: m for m, u in enumerate(scatter_units)}
 
@@ -570,38 +614,47 @@
         for i in range(PARTS):
             S[m, i % 2, i // 16, i // 8 % 2, i // 4 % 2, i // 2 % 2] = wire(grad[ROWS * i : ROWS * i + ROWS])
 
-    def ffn_back(q):
+    def up_back(q):
         cols = pl.ds(pl.multiple_of(D * q, D), D)
-        fg = f_grad[...]
-        pre = (dot(fg, down_block(q), 1, 1) * slope_g[:, cols].astype(f32)).astype(bf)
+        pre = (dot(f_grad[...], down_block(q), 1, 1) * slope_g[:, cols].astype(f32)).astype(bf)
+        slope_g[:, cols] = pre
+        put(message[UP_UNIT] + q, dot(nl_g[...], pre, 0, 0))
+
+    def down_back(q):
+        cols = pl.ds(pl.multiple_of(D * q, D), D)
+        pre = slope_g[:, cols]
         vgrad[pl.ds(5 + q, 1), :] = col_sum(pre)
-        put(message[UP_UNIT] + q, dot(nl_g[...], pre, 0, 0))
-        d_two[...] += dot(pre, unit(UP_UNIT + q), 1, 1)
-        down = dot(act_g[:, cols], fg, 0, 0)
+        acc_g[...] += dot(pre, unit(UP_UNIT + q), 1, 1)
+        down = dot(act_g[:, cols], f_grad[...], 0, 0)
         for i in range(8):
             for t in range(4):
                 at = 96 * i + ROWS * t
                 S[message[DOWN_UNIT] + t, i % 2, q // 2, q % 2, i // 4, i // 2 % 2] = wire(down[at : at + ROWS])
 
-    plan.loop(4, ffn_back)
+    plan.loop(4, up_back)
+    plan.loop(4, down_back)
     plan.before()
-    rhat, rstd = norm(r1_g[...])
-    g = d_two[...]
+    rhat, rstd = norm(res_g[...])
+    g = acc_g[...]
     vgrad[3:4, :] = col_sum(g * rhat)
     vgrad[4:5, :] = col_sum(g)
     one = norm_back(g * bias(3), rhat, rstd)
-    d_one[...] = one
-    a_grad[...] = one.astype(bf)
-    vgrad[2:3, :] = col_sum(a_grad[...])
-    put(message[OUT_UNIT], dot(ctx_gt[...], a_grad[...], 1, 0))
-    c_grad[...] = dot(a_grad[...], unit(OUT_UNIT), 1, 1).astype(bf)
+    res_g[...] = one
+    f_grad[...] = one.astype(bf)
+    vgrad[2:3, :] = col_sum(f_grad[...])
+    put(message[OUT_UNIT], dot(ctx_gt[...], f_grad[...], 1, 0))
+    nl_g[...] = dot(f_grad[...], unit(OUT_UNIT), 1, 1).astype(bf)
 
     slot_lane = lax.broadcasted_iota(jnp.int32, (PMAX, 128), 1)
 
     def attend_back(it):
+        for k in range(2):
+            pair_back(2 * it + k)
+
+    def pair_back(it):
         s, rows, cols, mask = pair_at(it)
         slots = pl.ds(pl.multiple_of(s * PMAX, PMAX), PMAX)
-        q, g = q_g[slots, cols], c_grad[slots, cols]
+        q, g = q_g[slots, cols], nl_g[slots, cols]
         k, v = J[1, rows, cols] * scale, J[2, rows, cols]
         none = jnp.zeros_like(q)
         both = lambda t: jnp.concatenate(
@@ -623,7 +676,7 @@
         J[1, rows, cols] = dk.astype(bf)
         J[2, rows, cols] = dv.astype(bf)
 
-    plan.loop(12, attend_back)
+    plan.loop(6, attend_back)
     plan.before()
     put(message[V_UNIT], dot(xs[...], J[2], 0, 0))
     vgrad[1:2, :] = col_sum(J[2])
@@ -638,36 +691,37 @@
 
     def ffn_all(it):
         t, q = it // 4, it % 4
-        rows = pl.ds(pl.multiple_of(256 * t, 256), 256)
+        rows = pl.ds(pl.multiple_of(512 * t, 512), 512)
 
         @pl.when(q == 0)
         def _():
             r = xs[rows, :].astype(f32) + (dot(ctx_t[:, rows], unit(OUT_UNIT), 0, 0) + bias(2))
             n = norm(r)[0] * bias(3) + bias(4)
-            n1_t[...] = n
             nl_t[...] = n.astype(bf)
             acc[...] = n + bias(9)
 
-        a = gelu_parts(dot(nl_t[...], unit(UP_UNIT + q), 1, 0) + bias(5 + q))[0]
-        acc[...] += dot(a.astype(bf), down_block(q), 1, 0)
+        half = [slice(0, 256), slice(256, 512)]
+        up = [dot(nl_t[h, :], unit(UP_UNIT + q), 1, 0) + bias(5 + q) for h in half]
+        for h, u in zip(half, up):
+            acc[h, :] += dot((u * normal_cdf(u)).astype(bf), down_block(q), 1, 0)
 
         @pl.when(q == 3)
         def _():
-            done = pltpu.make_async_copy(out_t, layer_out.at[rows, :], out_sem.at[0])
+            done = pltpu.make_async_copy(out_t.at[0:512], layer_out.at[rows, :], out_sem.at[0])
 
             @pl.when(t > 0)
             def _():
                 done.wait()
 
-            out_t[...] = (norm(acc[...])[0] * bias(10) + bias(11)).astype(bf)
+            out_t[:512, :] = (norm(acc[...])[0] * bias(10) + bias(11)).astype(bf)
             done.start()
 
-    plan.loop(16, ffn_all)
+    plan.loop(8, ffn_all)
 
     def grad_in(s):
         rows = pl.ds(pl.multiple_of(s * SEQ_LEN, SEQ_LEN), SEQ_LEN)
         slots = pl.ds(pl.multiple_of(s * PMAX, PMAX), PMAX)
-        t = d_one[slots, :] + dot(dq_g[slots, :], unit(Q_UNIT), 1, 1)
+        t = res_g[slots, :] + dot(dq_g[slots, :], unit(Q_UNIT), 1, 1)
         high = t.astype(bf)
         low = (t - high.astype(f32)).astype(bf)
         total = dot(pick_t[s], high, 1, 0) + dot(pick_t[s], low, 1, 0)
@@ -680,7 +734,7 @@
     store.start()
     plan.rest()
     g_vec[...] = vsum[z1, z0, y]
-    pltpu.make_async_copy(out_t, layer_out.at[0:256, :], out_sem.at[0]).wait()
+    pltpu.make_async_copy(out_t.at[0:512], layer_out.at[0:512, :], out_sem.at[0]).wait()
     store.wait()
     for copy in pair:
         copy.wait_send()
@@ -711,40 +765,34 @@
         in_specs=[smem, smem] + [vmem] * 2 + [hbm] * 6,
         out_specs=(hbm,) * 2 + (vmem,) * 5,
         scratch_shapes=[
-            pltpu.VMEM((UNITS, 2, 2, 2, 2, 2 * ROWS, D), bf),
+            pltpu.VMEM((DOWN_UNIT, 2, 2, 2, 2, 2 * ROWS, D), bf),
+            pltpu.VMEM((2, 2, 2, 2, 4, 2 * ROWS, D), bf),
             pltpu.VMEM((UNITS, 2, 2, 2, 2, 2, 16, WIRE), bf),
             pltpu.VMEM((UNITS, 2, 2, 2, 2, 16, WIRE), bf),
+            pltpu.VMEM((UNITS, 2, 2, 2, 16, WIRE), bf),
             pltpu.VMEM((tokens, D), bf),
             pltpu.VMEM((3, tokens, D), bf),
             pltpu.VMEM((D, tokens), bf),
             pltpu.VMEM((slots, FF), bf),
             pltpu.VMEM((slots, FF), bf),
             pltpu.VMEM((2, SEQ_LEN, PMAX), bf),
-            pltpu.VMEM((2, PMAX, SEQ_LEN), bf),
             pltpu.VMEM((slots, D), bf),
-            pltpu.VMEM((slots, D), bf),
-            pltpu.VMEM((slots, D), f32),
-            pltpu.VMEM((slots, D), f32),
             pltpu.VMEM((slots, D), bf),
             pltpu.VMEM((slots, D), f32),
             pltpu.VMEM((slots, D), f32),
             pltpu.VMEM((slots, D), bf),
             pltpu.VMEM((slots, D), bf),
             pltpu.VMEM((slots, D), bf),
-            pltpu.VMEM((slots, D), bf),
             pltpu.VMEM((D, slots), bf),
-            pltpu.VMEM((256, D), f32),
-            pltpu.VMEM((256, D), f32),
-            pltpu.VMEM((256, D), bf),
-            pltpu.VMEM((256, D), bf),
-            pltpu.VMEM((slots, D), bf),
-            pltpu.VMEM((2, 1728, 128), bf),
-            pltpu.VMEM((2, 1728, 128), f32),
+            pltpu.VMEM((512, D), f32),
+            pltpu.VMEM((512, D), bf),
+            pltpu.VMEM((576, D), bf),
+            pltpu.VMEM((2, 576, 128), f32),
             pltpu.VMEM((2, 2, 2, 2, 2, 16, 128), bf),
             pltpu.VMEM((16, D), f32),
             pltpu.VMEM((16, D), f32),
             pltpu.VMEM((2, 2, 2, 16, 128), f32),
-            pltpu.VMEM((5, 2, 2, 2, 16, 128), f32),
+            pltpu.VMEM((3, 2, 2, 2, 16, 128), f32),
             dma((UNITS, 7)),
             dma((UNITS, 7)),
             dma((UNITS, 7)),
@@ -762,10 +810,19 @@
     )(*args)
 
 
+settle_parts = 2
+
+
 def settle_kernel(n, *refs):
     ins, outs, held, sems = refs[:n], refs[n : 2 * n], refs[2 * n : 3 * n], refs[-1]
-    loads = [pltpu.make_async_copy(ins[i], held[i], sems.at[i]) for i in range(n)]
-    stores = [pltpu.make_async_copy(held[i], outs[i], sems.at[n + i]) for i in range(n)]
+    loads, stores = [], []
+    for i in range(n):
+        size = ins[i].shape[0] // settle_parts
+        for k in range(settle_parts):
+            rows = slice(size * k, size * k + size)
+            j = settle_parts * i + k
+            loads.append(pltpu.make_async_copy(ins[i].at[rows], held[i].at[rows], sems.at[0, j]))
+            stores.append(pltpu.make_async_copy(held[i].at[rows], outs[i].at[rows], sems.at[1, j]))
     for load in loads:
         load.start()
     for load, store in zip(loads, stores):
@@ -784,7 +841,7 @@
         in_specs=[pl.BlockSpec(memory_space=pl.ANY)] * n,
         out_specs=[hbm] * n,
         scratch_shapes=[pltpu.VMEM(a.shape, a.dtype) for a in arrays]
-        + [pltpu.SemaphoreType.DMA((2 * n,))],
+        + [pltpu.SemaphoreType.DMA((2, settle_parts * n))],
         compiler_params=pltpu.CompilerParams(vmem_limit_bytes=63 * 2**20),
     )(*arrays)
 

time: 159 us -> 145 us (0.912)
  Pallas kernels: 155 us -> 141 us
    pallas_call x1, Pallas kernels: 152 us -> 138 us  [layer_call(): pl.pallas_call(partial(layer_kernel, sizes), out_shape=(jax.ShapeDtypeStr...]
where the time goes in v4:
time: 145 us
  Pallas kernels  141 us (97%)
  local copies, waits for them, and re-layouts  2.83 us (2%)
    pallas_call x1, Pallas kernels, layer_call(): pl.pallas_call(partial(layer_kernel, sizes), out_shape=(jax.ShapeDtypeStr...  138 us
    pallas_call x1, Pallas kernels, settle(): pl.pallas_call(partial(settle_kernel, n), out_shape=[jax.ShapeDtypeStruct...  3.29 us

profile of v4, /device:TPU:0, one launch (start us, length us, event | category | flops | bytes accessed | tf_op | source)
XLA Modules:
  0.0 144.9 jit_solution(1522487829068284634)
XLA Ops:
  0.7 0.9 dynamic_update_slice.3
  1.5 0.0 copy-start
  1.5 0.6 copy-done
  2.1 138.1 %shard_map.153 = (bf16[1024,768]{1,0:T(8,128)(2,1)}, bf16[1024,768]{1,0:T(8,128)(2,1)}, f32[432,128]{1,0:T(8,128)}, f32[144,128]{1,0:T(8,128)}, f32[576,128]{1,0...) custom-call(s32[2]{0:T(128)} %lengths.1, s32[2]{0:T(128)} %counts.1, s32[2,128]{1,0:T(2,128)} %positions.1, ...), custom_call_target="tpu_custom_call" | custom-call | tf_op jit(solution)/shard_map/pallas_call | solution.py:754
  140.3 3.3 %shard_map.154 = (bf16[1024,768]{1,0:T(8,128)(2,1)}, bf16[1024,768]{1,0:T(8,128)(2,1)}, f32[432,128]{1,0:T(8,128)}, f32[144,128]{1,0:T(8,128)}, f32[576,128]{1,0:T(8,128)}, /*index=5*/f32[576,128]{1,0:T(8,128)}) custom-call(bf16[1024,768]{1,0:T(8,128)(2,1)} %get-tuple-element.20.refs_0_, bf16[1024,768]{1,0:T(8,128)(2,1)} %get-tuple-element.21.refs_1_, ...), custom_call_target="tpu_custom_call" | custom-call | tf_op jit(solution)/shard_map/pallas_call | solution.py:838
  143.6 1.4 dynamic_slice.3
  (1 shorter events, 0.0 us)
Async XLA Ops:
  1.5 0.6 copy-start

commit v5 on v4

--- a/solution.py
+++ b/solution.py
@@ -29,37 +29,37 @@
 WIRE = 3 * HALF
 
 gather_types = (
-    "ab", "ab", "ab", "ab", "ab", "gx", "gx", "ab", "ab", "ab", "ab", "gy",
+    "ab", "ab", "ab", "ab", "gx", "ab", "gy", "ab", "ab", "gx", "ab", "ab",
 )
 gather_order = (
-    "1z1", "12v0", "0z1", "5s0", "12v1", "2z1", "6s0", "9z1", "11s0", "1z0", "5s1", "12v2", "11s1",
-    "6s1", "0z0", "2z0", "1A1", "1B1", "0A1", "9z0", "0B1", "12v3", "8z1", "4z1", "10z1", "2A1",
-    "2B1", "0B2", "7z1", "0A2", "3z1", "4z0", "8z0", "12v4", "1A2", "1B2", "0C", "3z0", "2B2",
-    "7z0", "5z1", "2A2", "10z0", "4B1", "8B1", "4A1", "12v5", "1C", "3B1", "3A1", "8A1", "6z1",
-    "9A1", "2C", "9B1", "7B1", "4B2", "4A2", "11z1", "10A1", "8A2", "10B1", "5z0", "7A1", "3A2",
-    "6z0", "3B2", "9A2", "8B2", "4C", "9B2", "7A2", "7B2", "10A2", "3C", "10B2", "11z0", "5C",
-    "6C", "9C", "7C", "8C", "10C", "11C",
+    "12v0", "0z1", "1z1", "12v1", "4s0", "6s0", "2z1", "9s0", "12v2", "5z1", "0z0", "4s1", "12v3",
+    "6s1", "1z0", "9s1", "0B1", "3z1", "0A1", "2z0", "5z0", "1B1", "7z1", "1A1", "0B2", "0A2",
+    "3z0", "2B1", "2A1", "8z1", "1B2", "10z1", "7z0", "11z1", "12v4", "1A2", "3A1", "0C", "2B2",
+    "8z0", "10z0", "5A1", "5B1", "11z0", "2A2", "1C", "4z1", "3B1", "12v5", "6z1", "8B1", "10A1",
+    "2C", "7B1", "8A1", "10B1", "7A1", "11A1", "9z1", "4z0", "11B1", "8B2", "3A2", "3B2", "5A2",
+    "5B2", "6z0", "8A2", "7B2", "7A2", "11B2", "11A2", "10A2", "9z0", "3C", "5C", "4C", "10B2",
+    "6C", "7C", "8C", "11C", "10C", "9C",
 )
 gather_counts = (
-    0, 2, 1, 4, 35, 0, 4, 5, 3, 2, 0, 2, 2, 0, 0, 0, 4, 3, 3, 1, 0, 1, 1, 0, 0, 4, 0, 2, 1, 1, 1,
-    2,
+    1, 1, 2, 3, 25, 16, 1, 1, 1, 0, 1, 3, 3, 1, 3, 3, 0, 3, 2, 0, 0, 4, 1, 0, 0, 2, 3, 0, 1, 1, 1,
+    1,
 )
 scatter_units = (4, 5, 6, 7, 8, 9, 10, 11, 3, 1, 0, 2)
 scatter_types = (
-    "gx", "ab", "gy", "ab", "gx", "ab", "ab", "ab", "ab", "ab", "ab", "ab",
+    "gx", "ab", "gy", "ab", "ab", "gx", "ab", "ab", "ab", "ab", "ab", "ab",
 )
 scatter_order = (
-    "0C", "1C", "3C", "2C", "0z0", "1B2", "1A2", "3B2", "6C", "3A2", "5C", "2z0", "1A1", "7C",
-    "6A2", "4C", "6B2", "8C", "1B1", "0z1", "7A2", "7B2", "8A2", "5B2", "4z0", "3B1", "6A1", "8B2",
-    "2z1", "5A2", "3A1", "9C", "7A1", "7B1", "12v0", "4z1", "12v1", "5B1", "6B1", "10C", "9A2",
-    "8A1", "5A1", "3z0", "7z0", "8B1", "11C", "10B2", "1z0", "9B2", "10A2", "12v2", "5z0", "3z1",
-    "9A1", "6z0", "11A2", "9B1", "11B2", "8z0", "5z1", "10B1", "1z1", "10A1", "6z1", "12v3", "2s1",
-    "11B1", "4s1", "9z0", "8z1", "11A1", "0s1", "7z1", "12v4", "10z0", "11z0", "2s0", "9z1", "0s0",
-    "6L", "10z1", "4s0", "11z1", "3L", "2L", "0L", "9L", "1L", "5L", "7L", "12v5", "8L", "4L",
-    "10L", "11L",
+    "0C", "1C", "2C", "3C", "0z0", "1A2", "1B2", "3B2", "3A2", "4C", "6C", "2z0", "7C", "1B1",
+    "5C", "1A1", "8C", "4B2", "6A2", "3A1", "6B2", "7A2", "0z1", "5z0", "8B2", "4A2", "2z1", "3B1",
+    "7B2", "4B1", "9C", "8A2", "6A1", "11C", "4A1", "12v0", "6B1", "11B2", "11A2", "12v1", "1z0",
+    "5z1", "0s1", "7B1", "7A1", "3z0", "8A1", "11B1", "10C", "9A2", "6z0", "9B2", "11A1", "8B1",
+    "7z0", "10A2", "4z0", "12v2", "1z1", "3z1", "10B2", "6z1", "9A1", "0s0", "9B1", "2s1", "4z1",
+    "8z0", "11z0", "7z1", "10A1", "6L", "5s1", "4L", "12v3", "10B1", "0L", "8z1", "3L", "9z0",
+    "11z1", "2s0", "10z0", "1L", "12v4", "7L", "5s0", "8L", "9z1", "10z1", "2L", "11L", "5L", "9L",
+    "12v5", "10L",
 )
 scatter_counts = (
-    0, 1, 1, 0, 1, 4, 0, 1, 2, 9, 1, 2, 2, 1, 1, 2, 2, 4, 1, 8, 5, 4, 4, 5, 5, 8, 2, 7,
+    0, 1, 1, 1, 0, 4, 0, 0, 6, 4, 4, 4, 1, 0, 3, 1, 1, 2, 4, 4, 6, 7, 6, 10, 0, 11, 8, 1,
 )
 
 
@@ -648,33 +648,32 @@
     slot_lane = lax.broadcasted_iota(jnp.int32, (PMAX, 128), 1)
 
     def attend_back(it):
-        for k in range(2):
-            pair_back(2 * it + k)
-
-    def pair_back(it):
-        s, rows, cols, mask = pair_at(it)
-        slots = pl.ds(pl.multiple_of(s * PMAX, PMAX), PMAX)
-        q, g = q_g[slots, cols], nl_g[slots, cols]
-        k, v = J[1, rows, cols] * scale, J[2, rows, cols]
-        none = jnp.zeros_like(q)
-        both = lambda t: jnp.concatenate(
-            [jnp.where(slot_lane < HD, t, none), jnp.where(slot_lane < HD, none, t)], 0
-        )
-        q2, g2 = both(q), both(g)
+        at = [pair_at(2 * it + k) for k in range(2)]
+        none = jnp.zeros((PMAX, 128), bf)
         ones = jnp.full((2 * PMAX, 128), 1 / 128, bf)
-        scores = dot(jnp.concatenate([k, mask], 1), jnp.concatenate([q2, ones], 1), 1, 1)
-        e = jnp.exp(scores - jnp.max(scores, 0, keepdims=True))
-        probs = e * (1.0 / jnp.sum(e, 0, keepdims=True))
-        d_probs = dot(v, g2, 1, 1)
-        row_dot = jnp.sum(probs * d_probs, 0, keepdims=True)
-        d_scores = (probs * (d_probs - row_dot)).astype(bf)
-        dv = dot(probs.astype(bf), g2, 1, 0)
-        dk = dot(d_scores, q2 * scale, 1, 0)
-        dq2 = dot(d_scores, k, 0, 0)
-        dq = jnp.where(slot_lane < HD, dq2[:PMAX], dq2[PMAX:])
-        dq_g[slots, cols] = dq.astype(bf)
-        J[1, rows, cols] = dk.astype(bf)
-        J[2, rows, cols] = dv.astype(bf)
+
+        def both(t):
+            parts = [jnp.where(slot_lane < HD, t, none), jnp.where(slot_lane < HD, none, t)]
+            return jnp.concatenate(parts, 0)
+
+        slots = [pl.ds(pl.multiple_of(s * PMAX, PMAX), PMAX) for s, _, _, _ in at]
+        q2 = [both(q_g[sl, cols]) for sl, (_, _, cols, _) in zip(slots, at)]
+        g2 = [both(nl_g[sl, cols]) for sl, (_, _, cols, _) in zip(slots, at)]
+        keys = [J[1, rows, cols] * scale for _, rows, cols, _ in at]
+        scores = [
+            dot(jnp.concatenate([k, a[3]], 1), jnp.concatenate([q, ones], 1), 1, 1)
+            for k, q, a in zip(keys, q2, at)
+        ]
+        d_probs = [dot(J[2, rows, cols], g, 1, 1) for g, (_, rows, cols, _) in zip(g2, at)]
+        for i, (_, rows, cols, _) in enumerate(at):
+            e = jnp.exp(scores[i] - jnp.max(scores[i], 0, keepdims=True))
+            probs = e * (1.0 / jnp.sum(e, 0, keepdims=True))
+            row_dot = jnp.sum(probs * d_probs[i], 0, keepdims=True)
+            d_scores = (probs * (d_probs[i] - row_dot)).astype(bf)
+            J[2, rows, cols] = dot(probs.astype(bf), g2[i], 1, 0).astype(bf)
+            J[1, rows, cols] = dot(d_scores, q2[i] * scale, 1, 0).astype(bf)
+            dq2 = dot(d_scores, keys[i], 0, 0)
+            dq_g[slots[i], cols] = jnp.where(slot_lane < HD, dq2[:PMAX], dq2[PMAX:]).astype(bf)
 
     plan.loop(6, attend_back)
     plan.before()

time: 145 us -> 145 us (level)
  no operation moved by 1% of the time
where the time goes in v5:
time: 145 us
  Pallas kernels  141 us (97%)
  local copies, waits for them, and re-layouts  2.83 us (2%)
    pallas_call x1, Pallas kernels, layer_call(): pl.pallas_call(partial(layer_kernel, sizes), out_shape=(jax.ShapeDtypeStr...  138 us
    pallas_call x1, Pallas kernels, settle(): pl.pallas_call(partial(settle_kernel, n), out_shape=[jax.ShapeDtypeStruct...  3.29 us

profile of v5, /device:TPU:0, one launch (start us, length us, event | category | flops | bytes accessed | tf_op | source)
XLA Modules:
  0.0 144.6 jit_solution(16471195566120196164)
XLA Ops:
  0.7 0.9 dynamic_update_slice.3
  1.5 0.0 copy-start
  1.5 0.6 copy-done
  2.1 137.8 %shard_map.153 = (bf16[1024,768]{1,0:T(8,128)(2,1)}, bf16[1024,768]{1,0:T(8,128)(2,1)}, f32[432,128]{1,0:T(8,128)}, f32[144,128]{1,0:T(8,128)}, f32[576,128]{1,0...) custom-call(s32[2]{0:T(128)} %lengths.1, s32[2]{0:T(128)} %counts.1, s32[2,128]{1,0:T(2,128)} %positions.1, ...), custom_call_target="tpu_custom_call" | custom-call | tf_op jit(solution)/shard_map/pallas_call | solution.py:753
  139.9 3.3 %shard_map.154 = (bf16[1024,768]{1,0:T(8,128)(2,1)}, bf16[1024,768]{1,0:T(8,128)(2,1)}, f32[432,128]{1,0:T(8,128)}, f32[144,128]{1,0:T(8,128)}, f32[576,128]{1,0:T(8,128)}, /*index=5*/f32[576,128]{1,0:T(8,128)}) custom-call(bf16[1024,768]{1,0:T(8,128)(2,1)} %get-tuple-element.20.refs_0_, bf16[1024,768]{1,0:T(8,128)(2,1)} %get-tuple-element.21.refs_1_, ...), custom_call_target="tpu_custom_call" | custom-call | tf_op jit(solution)/shard_map/pallas_call | solution.py:837
  143.2 1.4 dynamic_slice.3
  (1 shorter events, 0.0 us)
Async XLA Ops:
  1.5 0.6 copy-start

commit v6 on v5

--- a/solution.py
+++ b/solution.py
@@ -809,15 +809,16 @@
     )(*args)
 
 
-settle_parts = 2
+settle_parts = 4
 
 
 def settle_kernel(n, *refs):
     ins, outs, held, sems = refs[:n], refs[n : 2 * n], refs[2 * n : 3 * n], refs[-1]
     loads, stores = [], []
     for i in range(n):
-        size = ins[i].shape[0] // settle_parts
-        for k in range(settle_parts):
+        parts = settle_parts if ins[i].shape[0] >= 1024 else 1
+        size = ins[i].shape[0] // parts
+        for k in range(parts):
             rows = slice(size * k, size * k + size)
             j = settle_parts * i + k
             loads.append(pltpu.make_async_copy(ins[i].at[rows], held[i].at[rows], sems.at[0, j]))

time: 145 us -> 145 us (level)
  no operation moved by 1% of the time
where the time goes in v6:
time: 145 us
  Pallas kernels  142 us (98%)
  local copies, waits for them, and re-layouts  2.83 us (2%)
    pallas_call x1, Pallas kernels, layer_call(): pl.pallas_call(partial(layer_kernel, sizes), out_shape=(jax.ShapeDtypeStr...  138 us
    pallas_call x1, Pallas kernels, settle(): pl.pallas_call(partial(settle_kernel, n), out_shape=[jax.ShapeDtypeStruct...  3.73 us

profile of v6, /device:TPU:0, one launch (start us, length us, event | category | flops | bytes accessed | tf_op | source)
XLA Modules:
  0.0 145.0 jit_solution(14525758022714398862)
XLA Ops:
  0.7 0.9 dynamic_update_slice.3
  1.5 0.0 copy-start
  1.5 0.6 copy-done
  2.1 137.8 %shard_map.153 = (bf16[1024,768]{1,0:T(8,128)(2,1)}, bf16[1024,768]{1,0:T(8,128)(2,1)}, f32[432,128]{1,0:T(8,128)}, f32[144,128]{1,0:T(8,128)}, f32[576,128]{1,0...) custom-call(s32[2]{0:T(128)} %lengths.1, s32[2]{0:T(128)} %counts.1, s32[2,128]{1,0:T(2,128)} %positions.1, ...), custom_call_target="tpu_custom_call" | custom-call | tf_op jit(solution)/shard_map/pallas_call | solution.py:753
  139.9 3.7 %shard_map.154 = (bf16[1024,768]{1,0:T(8,128)(2,1)}, bf16[1024,768]{1,0:T(8,128)(2,1)}, f32[432,128]{1,0:T(8,128)}, f32[144,128]{1,0:T(8,128)}, f32[576,128]{1,0:T(8,128)}, /*index=5*/f32[576,128]{1,0:T(8,128)}) custom-call(bf16[1024,768]{1,0:T(8,128)(2,1)} %get-tuple-element.20.refs_0_, bf16[1024,768]{1,0:T(8,128)(2,1)} %get-tuple-element.21.refs_1_, ...), custom_call_target="tpu_custom_call" | custom-call | tf_op jit(solution)/shard_map/pallas_call | solution.py:838
  143.7 1.4 dynamic_slice.3
  (1 shorter events, 0.0 us)
Async XLA Ops:
  1.5 0.6 copy-start
